TPU v7x, 256 devices: a whole 4x4x8 slice. The times are simulated.
256 devices in a mesh: sess: 32 (over y, x, core), blk: 8 (over z).
Axes of the slice: x: 4, y: 4, z: 8, core: 2. Of those that a mesh axis runs over, the one named last changes fastest.
Arguments:
- velocity_old: float32 [3, 8, 8, 8, 32768], P(None, None, None, None, ('sess', 'blk')), may hold values from -6 to 6
- conductance: float32 [8, 8, 8, 32768], P(None, None, None, ('sess', 'blk')), may hold values from 0.3 to 3
- donor_rank: int32 [262144], P(('sess', 'blk')), may hold values from 0 to 31, as said below
- donor_elem: int32 [262144], P(('sess', 'blk')), may hold values from 0 to 127
- target_node: int32 [262144], P(('sess', 'blk')), may hold values from 0 to 65535
- iface_weights: float32 [3, 8, 262144], P(None, None, ('sess', 'blk')), may hold values from -2.5 to 2.5
Outputs:
- velocity_new: float32 [3, 8, 8, 8, 32768], P(None, None, None, None, ('sess', 'blk'))
- iface_values: float32 [3, 262144], P(None, ('sess', 'blk'))
Inputs may be any that keep to these rules, and one draw needn't show every extreme that they name: `donor_rank`: ranks below 21 form the background session, the others the inner session; every point's donor rank lies in the session other than its own device's. At most 128 points of one device name one donor rank. For each blk index, one rank of each session is named by exactly 128 points of every device of the other session at that blk index. `donor_elem`: indexes the elements of the donor device that has the point's blk index. `target_node`: indexes the nodes of the point's own device.
All inputs are finite; a program needn't handle non-finite values.
Results may differ from a plain program's by a relative error of at most 0.00013.
Values sent between devices are 32-bit elements; how exact they have to be, the bound alone decides.
No kernel may reach another device: no remote copies, remote signals or barrier semaphores. Data moves between devices by JAX's collectives and lax.ppermute only.
A program may use at most 128 MiB of HBM per device.

v0:
```python
import functools

import jax
import jax.numpy as jnp
from jax import lax
from jax.experimental import pallas as pl
from jax.experimental.pallas import tpu as pltpu
from jax.sharding import PartitionSpec as P

NPASS = 4
H_MASS = 1.0
H_STIFF = 4.0
OMEGA = 0.6
TAU = 8.0
PEERS = 32
BLOCKS = 8
BACKGROUND = 21
F32 = jnp.float32
BF16 = jnp.bfloat16
I32 = jnp.int32
NT = (((1,), (1,)), ((), ()))


def iota(shape, dim):
    return lax.broadcasted_iota(I32, shape, dim)


def lane_gather(values, index):
    return jnp.take_along_axis(values, index, axis=1)


def split2(values):
    high = values.astype(BF16)
    return high, (values - high.astype(F32)).astype(BF16)


def other_session():
    sess = lax.axis_index("sess")
    outer = sess < BACKGROUND
    first = jnp.where(outer, BACKGROUND, 0)
    last = jnp.where(outer, PEERS, BACKGROUND)
    return first, last


def pack_kernel(rank_ref, elem_ref, weight_ref, send_ref, pos_ref, low_ref, high_ref):
    rank_iota = iota((PEERS, 128), 0)
    row = iota((128, 256), 0)
    col = iota((128, 256), 1)
    upper = jnp.where((row < col) | (col >= 128), 1.0, 0.0).astype(BF16)
    hits = [rank_ref[r : r + 1, :] == rank_iota for r in range(8)]
    hot = jnp.concatenate([jnp.where(hit, 1.0, 0.0).astype(BF16) for hit in hits], axis=0)
    counts = jnp.dot(hot, upper, preferred_element_type=F32)
    offset = jnp.zeros((PEERS, 128), F32)
    pos_iota = iota((128, 128), 0)
    lane = iota((PEERS, 128), 1).astype(F32)
    at_slot, low, high = [], [], []
    for r in range(8):
        mine = counts[r * PEERS : (r + 1) * PEERS]
        place = jnp.where(hits[r], mine[:, :128] + offset, 0.0)
        pos = jnp.sum(place, axis=0, keepdims=True).astype(I32)
        offset = offset + mine[:, 128:]
        pos_ref[r : r + 1, :] = pos
        at_slot.append(jnp.where(pos == pos_iota, 1.0, 0.0).astype(BF16))
        low.append(jnp.where(hits[r], lane, 0.0).astype(BF16))
        high.append(jnp.where(hits[r], float(r), 0.0).astype(BF16))
    at_slot = jnp.concatenate(at_slot, axis=1)
    both = jnp.concatenate([jnp.concatenate(low, axis=1), jnp.concatenate(high, axis=1)], axis=0)
    inverse = lax.dot_general(both, at_slot, NT, preferred_element_type=F32)
    low_ref[...] = inverse[:PEERS].astype(I32)
    high_ref[...] = inverse[PEERS:].astype(I32)
    first, last = other_session()
    sub = iota((8, 128), 0)
    elems = elem_ref[...].astype(F32)

    def one_peer(peer, carry):
        index = jnp.broadcast_to(low_ref[pl.ds(peer, 1), :], (8, 128))
        part = jnp.broadcast_to(high_ref[pl.ds(peer, 1), :], (8, 128))
        for group in range(3):
            rows = slice(group * 8, group * 8 + 8)
            picked = lane_gather(weight_ref[rows, 0:128], index)
            for r in range(1, 8):
                other = lane_gather(weight_ref[rows, r * 128 : r * 128 + 128], index)
                picked = jnp.where(part == r, other, picked)
            send_ref[peer, rows, :] = picked
        ids = jnp.where(sub == part, lane_gather(elems, index), 0.0)
        send_ref[peer, 24:32, :] = jnp.broadcast_to(jnp.sum(ids, axis=0, keepdims=True), (8, 128))
        return carry

    lax.fori_loop(first, last, one_peer, 0)


def serve_kernel(recv_ref, v_ref, reply_ref):
    first, last = other_session()

    def one_peer(peer, carry):
        index = recv_ref[peer, 24:32, :].astype(I32)
        wz = [jnp.broadcast_to(recv_ref[peer, z : z + 1, :], (8, 128)) for z in range(8)]
        wy = [jnp.broadcast_to(recv_ref[peer, 8 + y : 9 + y, :], (8, 128)) for y in range(8)]
        wx = recv_ref[peer, 16:24, :]
        for c in range(3):
            total = jnp.zeros((8, 128), F32)
            for z in range(8):
                line = jnp.zeros((8, 128), F32)
                for y in range(8):
                    line = line + lane_gather(v_ref[c, z, y], index) * wy[y]
                total = total + line * wz[z]
            reply_ref[peer, c : c + 1, :] = jnp.sum(total * wx, axis=0, keepdims=True)
        return carry

    lax.fori_loop(first, last, one_peer, 0)


def finish_kernel(reply_ref, rank_ref, pos_ref, target_ref, value_ref, ends_ref):
    first, last = other_session()
    ranks = [jnp.broadcast_to(rank_ref[r : r + 1, :], (8, 128)) for r in range(8)]
    index = [jnp.broadcast_to(pos_ref[r : r + 1, :], (8, 128)) for r in range(8)]

    def one_peer(peer, sums):
        have = reply_ref[peer]
        return tuple(
            jnp.where(ranks[r] == peer, lane_gather(have, index[r]), sums[r]) for r in range(8)
        )

    sums = lax.fori_loop(first, last, one_peer, tuple(jnp.zeros((8, 128), F32) for _ in range(8)))
    values = jnp.concatenate(sums, axis=1)
    value_ref[...] = values[0:3]
    target = jnp.concatenate([target_ref[r : r + 1, :] for r in range(8)], axis=1)
    elem = target >> 9
    zx = ((target >> 6) & 7) * 8 + (target & 7)
    y2 = ((target >> 3) & 7) * 2
    key = jnp.where(elem == 127, y2, jnp.where(elem == 0, y2 + 1, -1))
    left = jnp.where(zx == iota((64, 1024), 0), 1.0, 0.0).astype(BF16)
    hit = key == iota((16, 1024), 0)
    rows = jnp.concatenate([jnp.where(hit, values[c : c + 1], 0.0) for c in range(3)], axis=0)
    rows = jnp.concatenate([rows, jnp.zeros((16, 1024), F32)], axis=0)
    high, low = split2(rows)
    both = jnp.concatenate([high, low], axis=0)
    out = lax.dot_general(left, both, NT, preferred_element_type=F32)
    ends_ref[...] = TAU * (out + pltpu.roll(out, 64, 1))


def ends_kernel(v_ref, c_ref, ends_ref):
    lane = iota((8, 128), 1)
    for z in range(8):
        block = jnp.zeros((8, 128), F32)
        for c in range(3):
            for y in range(8):
                i = c * 8 + y
                rolled = pltpu.roll(v_ref[c, z, y], 2 * i + 1, 1)
                block = jnp.where((lane >> 1) == i, rolled, block)
        ends_ref[z * 8 : z * 8 + 8, :] = block
        block = jnp.zeros((8, 128), F32)
        for y in range(8):
            rolled = pltpu.roll(c_ref[z, y], 2 * y + 1, 1)
            block = jnp.where((lane >> 1) == y, rolled, block)
        block = block + pltpu.roll(block, 16, 1) + pltpu.roll(block, 32, 1)
        ends_ref[64 + z * 8 : 72 + z * 8, :] = block


def main_kernel(v_ref, c_ref, value_ref, target_ref, out_ref, rhs_ref, buf_ref, w_ref, k_ref, kx_ref, dl_ref):
    lane = iota((8, 128), 1)
    sub = iota((8, 128), 0)
    target = jnp.concatenate([target_ref[r : r + 1, :] for r in range(8)], axis=1)
    elem = target >> 9
    node = target & 511
    left = jnp.where(node == iota((512, 1024), 0), 1.0, 0.0).astype(BF16)
    hit = elem == iota((128, 1024), 0)
    for c in range(3):
        high, low = split2(jnp.where(hit, TAU * value_ref[c : c + 1, :], 0.0))
        both = jnp.concatenate([high, low], axis=0)
        out = lax.dot_general(left, both, NT, preferred_element_type=F32)
        added = (out[:, :128] + out[:, 128:]).reshape(8, 8, 8, 128)
        rhs_ref[c] = H_MASS * v_ref[c] + added
    for z in range(8):
        for y in range(8):
            k = H_STIFF * c_ref[z, y]
            k_ref[z, y] = k
            kx_ref[z, y] = jnp.where(sub < 7, k, 0.0)
    for y in range(8):
        diags = []
        for z in range(8):
            kx = kx_ref[z, y]
            d = H_MASS + kx + pltpu.roll(kx, 1, 0)
            if z < 7:
                d = d + k_ref[z, y]
            if z > 0:
                d = d + k_ref[z - 1, y]
            if y < 7:
                d = d + k_ref[z, y]
            if y > 0:
                d = d + k_ref[z, y - 1]
            diags.append(d)
        dl_ref[0, y] = diags[0]
        dl_ref[1, y] = diags[7]
        bottom = diags[0] + jnp.where(lane > 0, pltpu.roll(diags[7], 1, 1), 0.0)
        top = diags[7] + jnp.where(lane < 127, pltpu.roll(diags[0], 127, 1), 0.0)
        diags[0], diags[7] = bottom, top
        for z in range(8):
            w_ref[z, y] = OMEGA / diags[z]

    def local_sum(src, c, z, y, v):
        kx = kx_ref[z, y]
        s = rhs_ref[c, z, y] + kx * pltpu.roll(v, 7, 0) + pltpu.roll(kx * v, 1, 0)
        if z < 7:
            s = s + k_ref[z, y] * src[c, z + 1, y]
        if z > 0:
            s = s + k_ref[z - 1, y] * src[c, z - 1, y]
        if y < 7:
            s = s + k_ref[z, y] * src[c, z, y + 1]
        if y > 0:
            s = s + k_ref[z, y - 1] * src[c, z, y - 1]
        return s

    def one_pass(src, dst):
        for y in range(8):
            for z in range(1, 7):
                for c in range(3):
                    v = src[c, z, y]
                    s = local_sum(src, c, z, y, v)
                    dst[c, z, y] = (1.0 - OMEGA) * v + w_ref[z, y] * s
            for c in range(3):
                v0 = src[c, 0, y]
                v7 = src[c, 7, y]
                r0 = local_sum(src, c, 0, y, v0) - dl_ref[0, y] * v0
                r7 = local_sum(src, c, 7, y, v7) - dl_ref[1, y] * v7
                s0 = r0 + jnp.where(lane > 0, pltpu.roll(r7, 1, 1), 0.0)
                s7 = r7 + jnp.where(lane < 127, pltpu.roll(r0, 127, 1), 0.0)
                dst[c, 0, y] = v0 + w_ref[0, y] * s0
                dst[c, 7, y] = v7 + w_ref[7, y] * s7

    one_pass(v_ref, buf_ref)
    one_pass(buf_ref, out_ref)
    one_pass(out_ref, buf_ref)
    one_pass(buf_ref, out_ref)


def edge_kernel(main_ref, own_ref, below_ref, above_ref, add_ref, add_below_ref, add_above_ref, out_ref):
    blk = lax.axis_index("blk")
    lane = iota((8, 128), 1)
    sub = iota((8, 128), 0)
    even = (lane & 1) == 0
    joined = (even & (blk < BLOCKS - 1)) | (jnp.logical_not(even) & (blk > 0))
    y_of = (lane >> 1) & 7

    def stack(own, below, above, offset):
        lower, upper = [], []
        for z in range(8):
            rows = slice(offset + z * 8, offset + z * 8 + 8)
            mine = own[rows, :]
            lower.append(jnp.where(even, mine, pltpu.roll(below[rows, :], 1, 1)))
            upper.append(jnp.where(even, pltpu.roll(above[rows, :], 127, 1), mine))
        return lower + upper

    v = stack(own_ref, below_ref, above_ref, 0)
    cond = stack(own_ref, below_ref, above_ref, 64)
    add = stack(add_ref, add_below_ref, add_above_ref, 0)
    rhs = [H_MASS * v[i] + add[i] for i in range(16)]
    k = [H_STIFF * cond[i] for i in range(16)]
    kz = [k[i] if i % 8 < 7 else None for i in range(16)]
    ky = [jnp.where(y_of < 7, k[i], 0.0) for i in range(16)]
    kx = [jnp.where(sub < 7, k[i], 0.0) for i in range(16)]
    diag = []
    for i in range(16):
        d = H_MASS + kx[i] + pltpu.roll(kx[i], 1, 0) + ky[i] + pltpu.roll(ky[i], 2, 1)
        if kz[i] is not None:
            d = d + kz[i]
        if i % 8 > 0:
            d = d + kz[i - 1]
        diag.append(d)
    d7, d8 = diag[7], diag[8]
    full = list(diag)
    full[7] = d7 + jnp.where(joined, d8, 0.0)
    full[8] = d8 + jnp.where(joined, d7, 0.0)
    w = [OMEGA / d for d in full]
    for _ in range(NPASS):
        r = []
        for i in range(16):
            s = rhs[i] + kx[i] * pltpu.roll(v[i], 7, 0) + pltpu.roll(kx[i] * v[i], 1, 0)
            s = s + ky[i] * pltpu.roll(v[i], 126, 1) + pltpu.roll(ky[i] * v[i], 2, 1)
            if kz[i] is not None:
                s = s + kz[i] * v[i + 1]
            if i % 8 > 0:
                s = s + kz[i - 1] * v[i - 1]
            r.append(s - diag[i] * v[i])
        r7, r8 = r[7], r[8]
        r[7] = r7 + jnp.where(joined, r8, 0.0)
        r[8] = r8 + jnp.where(joined, r7, 0.0)
        v = [v[i] + w[i] * r[i] for i in range(16)]
    for c in range(3):
        for y in range(8):
            i = c * 8 + y
            back = (128 - (2 * i + 1)) % 128
            for z in range(8):
                new = v[z] if z >= 4 else v[8 + z]
                where = lane == (127 if z >= 4 else 0)
                out_ref[c, z, y] = jnp.where(where, pltpu.roll(new, back, 1), main_ref[c, z, y])


def call(kernel, outs, args, scratch=(), limit=24, **kw):
    single = len(outs) == 1
    spec = pl.BlockSpec(memory_space=pltpu.VMEM)
    return pl.pallas_call(
        kernel,
        out_shape=outs[0] if single else outs,
        in_specs=[spec] * len(args),
        out_specs=spec if single else [spec] * len(outs),
        scratch_shapes=list(scratch),
        compiler_params=pltpu.CompilerParams(vmem_limit_bytes=limit * 1024 * 1024),
        **kw,
    )(*args)


def sds(*shape, dtype=F32):
    return jax.ShapeDtypeStruct(shape, dtype)


def body(velocity_old, conductance, donor_rank, donor_elem, target_node, iface_weights):
    rank = donor_rank.reshape(8, 128)
    elem = donor_elem.reshape(8, 128)
    target = target_node.reshape(8, 128)
    weights = iface_weights.reshape(24, 1024)
    send, pos = call(
        pack_kernel,
        [sds(PEERS, 32, 128), sds(8, 128, dtype=I32)],
        [rank, elem, weights],
        [pltpu.VMEM((PEERS, 128), I32), pltpu.VMEM((PEERS, 128), I32)],
    )
    up = [(i, (i + 1) % BLOCKS) for i in range(BLOCKS)]
    down = [(j, i) for i, j in up]
    recv = lax.all_to_all(send, "sess", 0, 0, tiled=True)
    own = call(ends_kernel, [sds(128, 128)], [velocity_old, conductance])
    below = lax.ppermute(own, "blk", up)
    above = lax.ppermute(own, "blk", down)
    reply = call(serve_kernel, [sds(PEERS, 8, 128)], [recv, velocity_old])
    reply = lax.all_to_all(reply, "sess", 0, 0, tiled=True)
    iface_values, add = call(
        finish_kernel, [sds(3, 1024), sds(64, 128)], [reply, rank, pos, target]
    )
    add_below = lax.ppermute(add, "blk", up)
    add_above = lax.ppermute(add, "blk", down)
    plane = (8, 8, 8, 128)
    main = call(
        main_kernel,
        [sds(3, *plane)],
        [velocity_old, conductance, iface_values, target],
        [
            pltpu.VMEM((3,) + plane, F32),
            pltpu.VMEM((3,) + plane, F32),
            pltpu.VMEM(plane, F32),
            pltpu.VMEM(plane, F32),
            pltpu.VMEM(plane, F32),
            pltpu.VMEM((2, 8, 8, 128), F32),
        ],
        limit=32,
    )
    field = call(
        edge_kernel,
        [sds(3, *plane)],
        [main, own, below, above, add, add_below, add_above],
    )
    return field, iface_values


def solution(mesh):
    in_specs = (
        P(None, None, None, None, ("sess", "blk")),
        P(None, None, None, ("sess", "blk")),
        P(("sess", "blk")),
        P(("sess", "blk")),
        P(("sess", "blk")),
        P(None, None, ("sess", "blk")),
    )
    out_specs = (P(None, None, None, None, ("sess", "blk")), P(None, ("sess", "blk")))
    return jax.shard_map(body, mesh=mesh, in_specs=in_specs, out_specs=out_specs, check_vma=False)
```

profile of v0, /device:TPU:1, one launch (start us, length us, event | category | flops | bytes accessed | tf_op | source)
XLA Modules:
  0.0 56.2 jit_solution(5941436717562229658)
XLA Ops:
  0.6 1.0 %copy-done.2 = f32[3,8,1024]{2,1,0:T(8,128)S(1)} copy-done((f32[3,8,1024]{2,1,0:T(8,128)S(1)}, f32[3,8,1024]{2,1,0:T(8,128)}, u32[]{:S(2)}) %copy-start.2) | copy-done | bytes 98328
  1.6 0.7 %copy-done.5 = s32[1024]{0:T(1024)S(1)} copy-done((s32[1024]{0:T(1024)S(1)}, s32[1024]{0:T(1024)}, u32[]{:S(2)}) %copy-start.5) | copy-done | bytes 4120
  2.3 0.7 %copy-done.7 = s32[1024]{0:T(1024)S(1)} copy-done((s32[1024]{0:T(1024)S(1)}, s32[1024]{0:T(1024)}, u32[]{:S(2)}) %copy-start.7) | copy-done | bytes 4120
  3.0 1.5 %shard_map.77 = (f32[32,32,128]{2,1,0:T(8,128)S(1)}, s32[8,128]{1,0:T(8,128)S(1)}) custom-call(s32[8,128]{1,0:T(8,128)S(1)} %bitcast.7, s32[8,128]{1,0:T(8,128)S(1)} %bitcast.9, f32[24,1024]{1,0:T(8,128)S(1)} %bitcast.4), custom_call_target="tpu_custom_call" | custom-call | tf_op jit(solution)/shard_map/pallas_call | solution.py:302
  4.5 20.8 %all_to_all.10.recv_ref = f32[32,32,128]{2,1,0:T(8,128)S(1)} all-to-all(f32[32,32,128]{2,1,0:T(8,128)S(1)} %get-tuple-element.6), channel_id=1, replica_groups=mesh['sess'=32,'blk'=8] {'sess'}, dimensions={0} | all-to-all | bytes 1048576 | tf_op jit(solution)/shard_map/all_to_all | solution.py:330
  25.2 0.0 copy-done
  25.2 3.8 %shard_map.78 = f32[32,8,128]{2,1,0:T(8,128)} custom-call(f32[32,32,128]{2,1,0:T(8,128)S(1)} %all_to_all.10.recv_ref, f32[3,8,8,8,128]{4,3,2,1,0:T(8,128)S(1)} %copy-done), custom_call_target="tpu_custom_call" | custom-call | tf_op jit(solution)/shard_map/pallas_call | solution.py:302
  29.1 6.7 %all-to-all-start.1 = ((f32[32,8,128]{2,1,0:T(8,128)}), f32[32,8,128]{2,1,0:T(8,128)S(1)}, u32[]{:S(2)}, u32[]{:S(2)}) async-start(f32[32,8,128]{2,1,0:T(8,128)} %shard_map.78), calls=%async_computation.1 | async-start | bytes 262144 | tf_op jit(solution)/shard_map/all_to_all | solution.py:335
  35.8 0.0 copy-start.4
  35.8 0.0 copy-start.6
  35.8 0.7 %shard_map.81.own_ref = f32[128,128]{1,0:T(8,128)S(1)} custom-call(f32[3,8,8,8,128]{4,3,2,1,0:T(8,128)S(1)} %copy-done, f32[8,8,8,128]{3,2,1,0:T(8,128)S(1)} %copy-done.1), custom_call_target="tpu_custom_call" | custom-call | tf_op jit(solution)/shard_map/pallas_call | solution.py:302
  36.5 5.7 %collective-permute-start.1 = (f32[128,128]{1,0:T(8,128)S(1)}, f32[128,128]{1,0:T(8,128)S(1)}, u32[]{:S(2)}, u32[]{:S(2)}) collective-permute-start(f32[128,128]{1,0:T(8,128)S(1)} %shard_map.81.own_ref), channel_id=1, source_target_pairs={{1,0},{2,1},{3,2},{4,3},{5,4},{6,5},{7,6},{0,7},{9,8},{10,9},{11,1... | collective-permute-start | bytes 196616 | tf_op jit(solution)/shard_map/ppermute | solution.py:333
  42.2 0.0 collective-permute-start
  42.2 1.3 %all-to-all-done.1.reply_ref = f32[32,8,128]{2,1,0:T(8,128)S(1)} async-done(((f32[32,8,128]{2,1,0:T(8,128)}), f32[32,8,128]{2,1,0:T(8,128)S(1)}, u32[]{:S(2)}, u32[]{:S(2)}) %all-to-all-start.1) | async-done | bytes 131104 | tf_op jit(solution)/shard_map/all_to_all | solution.py:335
  43.4 1.7 %shard_map.79 = (f32[3,1024]{1,0:T(4,128)}, f32[64,128]{1,0:T(8,128)S(1)}) custom-call(f32[32,8,128]{2,1,0:T(8,128)S(1)} %all-to-all-done.1.reply_ref, s32[8,128]{1,0:T(8,128)S(1)} %bitcast.8, s32[8,128]{1,0:T(8,128)S(1)} %get-tuple-element.7.pos_ref, s32[8,128]{1,0:T(8,128)S(1)} %bitcast.5), custom_call_target="tpu_custom_call" | custom-call | tf_op jit(solution)/shard_map/pallas_call | solution.py:302
  45.1 5.6 %collective-permute-start.3 = (f32[64,128]{1,0:T(8,128)S(1)}, f32[64,128]{1,0:T(8,128)S(1)}, u32[]{:S(2)}, u32[]{:S(2)}) collective-permute-start(f32[64,128]{1,0:T(8,128)S(1)} %get-tuple-element.9.add_ref), channel_id=1, source_target_pairs={{1,0},{2,1},{3,2},{4,3},{5,4},{6,5},{7,6},{0,7},{9,8},{10,9},{11,1... | collective-permute-start | bytes 98312 | tf_op jit(solution)/shard_map/ppermute | solution.py:340
  50.7 0.0 collective-permute-start.2
  50.7 0.7 %copy-done.3 = f32[3,1024]{1,0:T(4,128)S(1)} copy-done((f32[3,1024]{1,0:T(4,128)S(1)}, f32[3,1024]{1,0:T(4,128)}, u32[]{:S(2)}) %copy-start.3) | copy-done | bytes 12312
  51.4 3.0 %shard_map.80.main_ref = f32[3,8,8,8,128]{4,3,2,1,0:T(8,128)S(1)} custom-call(f32[3,8,8,8,128]{4,3,2,1,0:T(8,128)S(1)} %copy-done, f32[8,8,8,128]{3,2,1,0:T(8,128)S(1)} %copy-done.1, f32[3,1024]{1,0:T(4,128)S(1)} %copy-done.3, s32[8,128]{1,0:T(8,128)S(1)} %bitcast.6), custom_call_target="tpu_custom_call" | custom-call | tf_op jit(solution)/shard_map/pallas_call | solution.py:302
  54.5 0.0 collective-permute-done.1.above_ref
  54.5 0.0 collective-permute-done.below_ref
  54.5 0.0 collective-permute-done.3.add_above_ref
  54.5 0.2 collective-permute-done.2.add_below_ref
  54.7 1.6 %shard_map.82 = f32[3,8,8,8,128]{4,3,2,1,0:T(8,128)} custom-call(f32[3,8,8,8,128]{4,3,2,1,0:T(8,128)S(1)} %shard_map.80.main_ref, f32[128,128]{1,0:T(8,128)S(1)} %shard_map.81.own_ref, f32[128,128]{1,0:T(8,128)S(1)} %collective-permute-done.below_ref, f32[128,128]{1,0:T(8,128)S(1)} %collective-permute-done.1.above_ref, ...), custom_call_target="tpu_custom_call" | custom-call | tf_op jit(solution)/shard_map/pallas_call | solution.py:302
  (9 shorter events, 0.0 us)
Async XLA Ops:
  0.6 24.6 %copy-start = (f32[3,8,8,8,128]{4,3,2,1,0:T(8,128)S(1)}, f32[3,8,8,8,128]{4,3,2,1,0:T(8,128)}, u32[]{:S(2)}) copy-start(f32[3,8,8,8,128]{4,3,2,1,0:T(8,128)} %v_ref.5) | copy-start | bytes 2359300
  0.6 1.0 %copy-start.2 = (f32[3,8,1024]{2,1,0:T(8,128)S(1)}, f32[3,8,1024]{2,1,0:T(8,128)}, u32[]{:S(2)}) copy-start(f32[3,8,1024]{2,1,0:T(8,128)} %param.11) | copy-start | bytes 294916
  1.6 0.7 %copy-start.5 = (s32[1024]{0:T(1024)S(1)}, s32[1024]{0:T(1024)}, u32[]{:S(2)}) copy-start(s32[1024]{0:T(1024)} %param.8) | copy-start | bytes 12292
  2.3 0.7 %copy-start.7 = (s32[1024]{0:T(1024)S(1)}, s32[1024]{0:T(1024)}, u32[]{:S(2)}) copy-start(s32[1024]{0:T(1024)} %param.9) | copy-start | bytes 12292
  29.1 6.7 %copy-start.1 = (f32[8,8,8,128]{3,2,1,0:T(8,128)S(1)}, f32[8,8,8,128]{3,2,1,0:T(8,128)}, u32[]{:S(2)}) copy-start(f32[8,8,8,128]{3,2,1,0:T(8,128)} %c_ref.3) | copy-start | bytes 786436
  29.1 14.4 %all-to-all-start.1 = ((f32[32,8,128]{2,1,0:T(8,128)}), f32[32,8,128]{2,1,0:T(8,128)S(1)}, u32[]{:S(2)}, u32[]{:S(2)}) async-start(f32[32,8,128]{2,1,0:T(8,128)} %shard_map.78), calls=%async_computation.1 | async-start | bytes 262144 | tf_op jit(solution)/shard_map/all_to_all | solution.py:335
  35.8 7.6 %copy-start.4 = (s32[1024]{0:T(1024)S(1)}, s32[1024]{0:T(1024)}, u32[]{:S(2)}) copy-start(s32[1024]{0:T(1024)} %param.10) | copy-start | bytes 12292
  35.8 7.6 %copy-start.6 = (s32[1024]{0:T(1024)S(1)}, s32[1024]{0:T(1024)}, u32[]{:S(2)}) copy-start(s32[1024]{0:T(1024)} %param.8) | copy-start | bytes 12292
  36.5 17.9 %collective-permute-start.1 = (f32[128,128]{1,0:T(8,128)S(1)}, f32[128,128]{1,0:T(8,128)S(1)}, u32[]{:S(2)}, u32[]{:S(2)}) collective-permute-start(f32[128,128]{1,0:T(8,128)S(1)} %shard_map.81.own_ref), channel_id=1, source_target_pairs={{1,0},{2,1},{3,2},{4,3},{5,4},{6,5},{7,6},{0,7},{9,8},{10,9},{11,1... | collective-permute-start | bytes 196616 | tf_op jit(solution)/shard_map/ppermute | solution.py:333
  42.2 12.3 %collective-permute-start = (f32[128,128]{1,0:T(8,128)S(1)}, f32[128,128]{1,0:T(8,128)S(1)}, u32[]{:S(2)}, u32[]{:S(2)}) collective-permute-start(f32[128,128]{1,0:T(8,128)S(1)} %shard_map.81.own_ref), channel_id=1, source_target_pairs={{0,1},{1,2},{2,3},{3,4},{4,5},{5,6},{6,7},{7,0},{8,9},{9,10},{10,1... | collective-permute-start | bytes 196616 | tf_op jit(solution)/shard_map/ppermute | solution.py:332
  45.1 9.3 %collective-permute-start.3 = (f32[64,128]{1,0:T(8,128)S(1)}, f32[64,128]{1,0:T(8,128)S(1)}, u32[]{:S(2)}, u32[]{:S(2)}) collective-permute-start(f32[64,128]{1,0:T(8,128)S(1)} %get-tuple-element.9.add_ref), channel_id=1, source_target_pairs={{1,0},{2,1},{3,2},{4,3},{5,4},{6,5},{7,6},{0,7},{9,8},{10,9},{11,1... | collective-permute-start | bytes 98312 | tf_op jit(solution)/shard_map/ppermute | solution.py:340
  50.7 4.0 %collective-permute-start.2 = (f32[64,128]{1,0:T(8,128)S(1)}, f32[64,128]{1,0:T(8,128)S(1)}, u32[]{:S(2)}, u32[]{:S(2)}) collective-permute-start(f32[64,128]{1,0:T(8,128)S(1)} %get-tuple-element.9.add_ref), channel_id=1, source_target_pairs={{0,1},{1,2},{2,3},{3,4},{4,5},{5,6},{6,7},{7,0},{8,9},{9,10},{10,1... | collective-permute-start | bytes 98312 | tf_op jit(solution)/shard_map/ppermute | solution.py:339
  50.7 0.7 %copy-start.3 = (f32[3,1024]{1,0:T(4,128)S(1)}, f32[3,1024]{1,0:T(4,128)}, u32[]{:S(2)}) copy-start(f32[3,1024]{1,0:T(4,128)} %get-tuple-element.5.value_ref) | copy-start | bytes 36868
where the time goes:
time: 56.6 us; the launch traced here: 56.2 us
  blocking collectives  20.8 us (37%)
  starting transfers between devices  18 us (32%)
  Pallas kernels  12.3 us (22%)
  local copies, waits for them, and re-layouts  3.07 us (5%)
  waiting for transfers between devices  1.46 us (3%)
  between operations  0.71 us (1%)
    all_to_all x1, blocking collectives, body(): recv = lax.all_to_all(send, 'sess', 0, 0, tiled=True)  20.8 us
    pallas_call x6, Pallas kernels, call(): pl.pallas_call(kernel, out_shape=outs[0] if single else outs, in_specs=[s...  12.3 us
    all_to_all x1, starting transfers between devices, body(): reply = lax.all_to_all(reply, 'sess', 0, 0, tiled=True)  6.73 us
    ppermute x1, starting transfers between devices, body(): above = lax.ppermute(own, 'blk', down)  5.66 us
    ppermute x1, starting transfers between devices, body(): add_above = lax.ppermute(add, 'blk', down)  5.58 us
    unnamed x16, local copies, waits for them, and re-layouts  3.07 us
    all_to_all x1, waiting for transfers between devices, body(): reply = lax.all_to_all(reply, 'sess', 0, 0, tiled=True)  1.25 us
  transfers between devices with their start and end apart: 5, of which 2 were waited for; matrix products, arithmetic and copies ran while one was open for 0% of the time, Pallas kernels for 10%

commit v1 on v0

v1 whole, which is shorter than its diff:
```python
import jax
import jax.numpy as jnp
from jax import lax
from jax.experimental import pallas as pl
from jax.experimental.pallas import tpu as pltpu
from jax.sharding import PartitionSpec as P

NPASS = 4
H_MASS = 1.0
H_STIFF = 4.0
OMEGA = 0.6
TAU = 8.0
PEERS = 32
BLOCKS = 8
BACKGROUND = 21
F32 = jnp.float32
BF16 = jnp.bfloat16
I32 = jnp.int32
NT = (((1,), (1,)), ((), ()))


def iota(shape, dim):
    return lax.broadcasted_iota(I32, shape, dim)


def lane_gather(values, index):
    return jnp.take_along_axis(values, index, axis=1)


def split2(values):
    high = values.astype(BF16)
    return high, (values - high.astype(F32)).astype(BF16)


def pack_kernel(
    rank_hbm, elem_hbm, weight_hbm, target_hbm, send_ref, meta_ref, rank_ref, elem_ref, weight_ref, target_ref, low_ref, high_ref, sems
):
    copies = [
        pltpu.make_async_copy(rank_hbm, rank_ref, sems.at[0]),
        pltpu.make_async_copy(elem_hbm, elem_ref, sems.at[1]),
        pltpu.make_async_copy(weight_hbm, weight_ref, sems.at[2]),
        pltpu.make_async_copy(target_hbm, target_ref, sems.at[3]),
    ]
    for copy in copies:
        copy.start()
    copies[0].wait()
    rank_iota = iota((PEERS, 128), 0)
    row = iota((128, 256), 0)
    col = iota((128, 256), 1)
    upper = jnp.where((row < col) | (col >= 128), 1.0, 0.0).astype(BF16)
    hits = [rank_ref[r : r + 1, :] == rank_iota for r in range(8)]
    hot = jnp.concatenate([jnp.where(hit, 1.0, 0.0).astype(BF16) for hit in hits], axis=0)
    counts = jnp.dot(hot, upper, preferred_element_type=F32)
    offset = jnp.zeros((PEERS, 128), F32)
    pos_iota = iota((128, 128), 0)
    lane = iota((PEERS, 128), 1).astype(F32)
    at_slot, low, high = [], [], []
    for r in range(8):
        mine = counts[r * PEERS : (r + 1) * PEERS]
        place = jnp.where(hits[r], mine[:, :128] + offset, 0.0)
        pos = jnp.sum(place, axis=0, keepdims=True).astype(I32)
        offset = offset + mine[:, 128:]
        meta_ref[r : r + 1, :] = pos
        at_slot.append(jnp.where(pos == pos_iota, 1.0, 0.0).astype(BF16))
        low.append(jnp.where(hits[r], lane, 0.0).astype(BF16))
        high.append(jnp.where(hits[r], float(r), 0.0).astype(BF16))
    at_slot = jnp.concatenate(at_slot, axis=1)
    both = jnp.concatenate([jnp.concatenate(low, axis=1), jnp.concatenate(high, axis=1)], axis=0)
    inverse = lax.dot_general(both, at_slot, NT, preferred_element_type=F32)
    low_ref[...] = inverse[:PEERS].astype(I32)
    high_ref[...] = inverse[PEERS:].astype(I32)
    for copy in copies[1:]:
        copy.wait()
    meta_ref[8:16, :] = rank_ref[...]
    meta_ref[16:24, :] = target_ref[...]
    outer = lax.axis_index("sess") < BACKGROUND
    first = jnp.where(outer, BACKGROUND, 0)
    turns = jnp.where(outer, 1, 2)
    sub = iota((8, 128), 0)
    elems = elem_ref[...].astype(F32)

    def some_peers(turn, carry):
        for step in range(PEERS - BACKGROUND):
            peer = first + turn * (PEERS - BACKGROUND) + step
            index = jnp.broadcast_to(low_ref[pl.ds(peer, 1), :], (8, 128))
            part = jnp.broadcast_to(high_ref[pl.ds(peer, 1), :], (8, 128))
            for group in range(3):
                rows = slice(group * 8, group * 8 + 8)
                picked = lane_gather(weight_ref[rows, 0:128], index)
                for r in range(1, 8):
                    other = lane_gather(weight_ref[rows, r * 128 : r * 128 + 128], index)
                    picked = jnp.where(part == r, other, picked)
                send_ref[pl.ds(peer * 25 + group * 8, 8), :] = picked
            ids = jnp.where(sub == part, lane_gather(elems, index), 0.0)
            send_ref[pl.ds(peer * 25 + 24, 1), :] = jnp.sum(ids, axis=0, keepdims=True)
        return carry

    lax.fori_loop(0, turns, some_peers, 0)


def serve_kernel(recv_ref, split_ref, first_ref, reply_ref):
    outer = lax.axis_index("sess") < BACKGROUND
    first = jnp.where(outer, BACKGROUND - 1, 0)
    turns = jnp.where(outer, 3, 6)
    elem_iota = iota((128, 128), 0)

    def four_peers(turn, carry):
        peers = [first + turn * 4 + i for i in range(4)]
        hot, picks = [], []
        for peer in peers:
            index = recv_ref[pl.ds(peer * 25 + 24, 1), :].astype(I32)
            picks.append(jnp.broadcast_to(index, (8, 128)))
            hot.append(jnp.where(index == elem_iota, 1.0, 0.0).astype(BF16))
        hot = jnp.concatenate(hot, axis=1)
        hot = jnp.concatenate([hot, hot], axis=0)

        def weight(peer, i):
            return jnp.broadcast_to(recv_ref[pl.ds(peer * 25 + i, 1), :], (8, 128))

        for c in range(3):
            if c:
                rows = slice(c * 512 - 512, c * 512)
                picked = jnp.dot(split_ref[rows, :], hot, preferred_element_type=F32).reshape(8, 8, 8, 512)
            for i, peer in enumerate(peers):
                total = None
                for z in range(8):
                    line = None
                    for y in range(8):
                        if c:
                            term = picked[z, y, :, i * 128 : i * 128 + 128]
                        else:
                            term = lane_gather(first_ref[z, y], picks[i])
                        term = term * weight(peer, 8 + y)
                        line = term if line is None else line + term
                    line = line * weight(peer, z)
                    total = line if total is None else total + line
                wx = recv_ref[pl.ds(peer * 25 + 16, 8), :]
                reply_ref[pl.ds(peer * 3 + c, 1), :] = jnp.sum(total * wx, axis=0, keepdims=True)
        return carry

    lax.fori_loop(0, turns, four_peers, 0)


def finish_kernel(reply_ref, meta_ref, value_ref, copy_ref, low_ref, high_ref):
    sub = iota((8, 128), 0)
    planes = [[reply_ref[pl.ds(g * 24 + c, 8, stride=3), :] for g in range(4)] for c in range(3)]
    values = [[], [], []]
    for r in range(8):
        index = jnp.broadcast_to(meta_ref[r : r + 1, :], (8, 128))
        rank = jnp.broadcast_to(meta_ref[8 + r : 9 + r, :], (8, 128))
        for c in range(3):
            total = jnp.zeros((8, 128), F32)
            for g in range(4):
                total = jnp.where(rank == sub + 8 * g, lane_gather(planes[c][g], index), total)
            values[c].append(jnp.sum(total, axis=0, keepdims=True))
    values = jnp.concatenate([jnp.concatenate(v, axis=1) for v in values], axis=0)
    value_ref[...] = values
    copy_ref[...] = values
    target = jnp.concatenate([meta_ref[16 + r : 17 + r, :] for r in range(8)], axis=1)
    elem = target >> 9
    zx = ((target >> 6) & 7) * 8 + (target & 7)
    y2 = ((target >> 3) & 7) * 2
    key = jnp.where(elem == 127, y2, jnp.where(elem == 0, y2 + 1, -1))
    left = jnp.where(zx == iota((64, 1024), 0), 1.0, 0.0).astype(BF16)
    hit = key == iota((16, 1024), 0)
    rows = jnp.concatenate([jnp.where(hit, values[c : c + 1], 0.0) for c in range(3)], axis=0)
    rows = jnp.concatenate([rows, jnp.zeros((16, 1024), F32)], axis=0)
    high, low = split2(rows)
    both = jnp.concatenate([high, low], axis=0)
    out = lax.dot_general(left, both, NT, preferred_element_type=F32)
    out = TAU * (out + pltpu.roll(out, 64, 1))
    low_ref[...] = out[:32]
    high_ref[...] = out[32:]


def ends_kernel(v_ref, c_ref, ends_ref, split_ref, first_ref):
    first_ref[...] = v_ref[0]
    lane = iota((8, 128), 1)
    for c in (1, 2):
        high, low = split2(v_ref[c].reshape(512, 128))
        split_ref[c * 512 - 512 : c * 512, 0:128] = high
        split_ref[c * 512 - 512 : c * 512, 128:256] = low
    for z in range(8):
        block = jnp.zeros((8, 128), F32)
        for c in range(3):
            for y in range(8):
                i = c * 8 + y
                rolled = pltpu.roll(v_ref[c, z, y], 2 * i + 1, 1)
                block = jnp.where((lane >> 1) == i, rolled, block)
        ends_ref[z * 8 : z * 8 + 8, :] = block
        block = jnp.zeros((8, 128), F32)
        for y in range(8):
            rolled = pltpu.roll(c_ref[z, y], 2 * y + 1, 1)
            block = jnp.where((lane >> 1) == y, rolled, block)
        block = block + pltpu.roll(block, 16, 1) + pltpu.roll(block, 32, 1)
        ends_ref[64 + z * 8 : 72 + z * 8, :] = block


def neighbour_sum(c_ref, kx, src, c, z, y, v):
    s = kx * pltpu.roll(v, 7, 0) + pltpu.roll(kx * v, 1, 0)
    if z < 7:
        s = s + c_ref[z, y] * src[c, z + 1, y]
    if z > 0:
        s = s + c_ref[z - 1, y] * src[c, z - 1, y]
    if y < 7:
        s = s + c_ref[z, y] * src[c, z, y + 1]
    if y > 0:
        s = s + c_ref[z, y - 1] * src[c, z, y - 1]
    return s


def local_diag(c_ref, z, y):
    kx = jnp.where(iota((8, 128), 0) < 7, c_ref[z, y], 0.0)
    d = H_MASS / H_STIFF + kx + pltpu.roll(kx, 1, 0)
    if z < 7:
        d = d + c_ref[z, y]
    if z > 0:
        d = d + c_ref[z - 1, y]
    if y < 7:
        d = d + c_ref[z, y]
    if y > 0:
        d = d + c_ref[z, y - 1]
    return d


def couple(lower, upper, lane):
    to_upper = upper + jnp.where(lane > 0, pltpu.roll(lower, 1, 1), 0.0)
    to_lower = lower + jnp.where(lane < 127, pltpu.roll(upper, 127, 1), 0.0)
    return to_lower, to_upper


def one_pass(c_ref, w_ref, dl_ref, rhs, src, dst, extra=None):
    lane = iota((8, 128), 1)
    sub = iota((8, 128), 0)

    def store(c, z, y, value):
        dst[c, z, y] = value if extra is None else value + extra[c, z, y]

    for y in range(8):
        for z in range(1, 7):
            kx = jnp.where(sub < 7, c_ref[z, y], 0.0)
            for c in range(3):
                v = src[c, z, y]
                s = rhs(c, z, y) + neighbour_sum(c_ref, kx, src, c, z, y, v)
                store(c, z, y, (1.0 - OMEGA) * v + w_ref[z, y] * s)
        k0 = jnp.where(sub < 7, c_ref[0, y], 0.0)
        k7 = jnp.where(sub < 7, c_ref[7, y], 0.0)
        for c in range(3):
            v0 = src[c, 0, y]
            v7 = src[c, 7, y]
            r0 = rhs(c, 0, y) + neighbour_sum(c_ref, k0, src, c, 0, y, v0) - dl_ref[0, y] * v0
            r7 = rhs(c, 7, y) + neighbour_sum(c_ref, k7, src, c, 7, y, v7) - dl_ref[1, y] * v7
            s7, s0 = couple(r7, r0, lane)
            store(c, 0, y, v0 + w_ref[0, y] * s0)
            store(c, 7, y, v7 + w_ref[7, y] * s7)


def edge_masks():
    blk = lax.axis_index("blk")
    even = (iota((8, 128), 1) & 1) == 0
    joined = (even & (blk < BLOCKS - 1)) | (jnp.logical_not(even) & (blk > 0))
    return even, joined


def edge_stack(own, below, above, offset, even):
    lower, upper = [], []
    for z in range(8):
        rows = slice(offset + z * 8, offset + z * 8 + 8)
        mine = own[rows, :]
        lower.append(jnp.where(even, mine, pltpu.roll(below[rows, :], 1, 1)))
        upper.append(jnp.where(even, pltpu.roll(above[rows, :], 127, 1), mine))
    return lower + upper


def edge_pass(number, v, rhs, k, ky, kx, w, d7, d8, joined):
    r = {}
    for i in range(1 + number, 15 - number):
        s = rhs[i]
        s = s + kx[i] * pltpu.roll(v[i], 7, 0) + pltpu.roll(kx[i] * v[i], 1, 0)
        s = s + ky[i] * pltpu.roll(v[i], 126, 1) + pltpu.roll(ky[i] * v[i], 2, 1)
        if i % 8 < 7:
            s = s + k[i] * v[i + 1]
        if i % 8 > 0:
            s = s + k[i - 1] * v[i - 1]
        if i == 7:
            s = s - d7 * v[i]
        if i == 8:
            s = s - d8 * v[i]
        r[i] = s
    r[7], r[8] = r[7] + jnp.where(joined, r[8], 0.0), r[8] + jnp.where(joined, r[7], 0.0)
    return {i: (v[i] if i in (7, 8) else (1.0 - OMEGA) * v[i]) + w[i] * r[i] for i in r}


def base_kernel(v_ref, c_ref, meta_ref, out_ref, w_ref, node_ref, buf_ref, dl_ref):
    lane = iota((8, 128), 1)
    target = jnp.concatenate([meta_ref[16 + r : 17 + r, :] for r in range(8)], axis=1)
    node_ref[...] = jnp.where((target & 511) == iota((512, 1024), 0), 1.0, 0.0).astype(BF16)
    for y in range(8):
        diags = [local_diag(c_ref, z, y) for z in range(8)]
        dl_ref[0, y] = diags[0]
        dl_ref[1, y] = diags[7]
        diags[7], diags[0] = couple(diags[7], diags[0], lane)
        for z in range(8):
            w_ref[z, y] = OMEGA / diags[z]

    def rhs(c, z, y):
        return (H_MASS / H_STIFF) * v_ref[c, z, y]

    coefs = (c_ref, w_ref, dl_ref, rhs)
    one_pass(*coefs, v_ref, buf_ref)
    one_pass(*coefs, buf_ref, out_ref)
    one_pass(*coefs, out_ref, buf_ref)
    one_pass(*coefs, buf_ref, out_ref)


def main_kernel(value_ref, meta_ref, node_ref, base_ref, w_ref, c_ref, out_ref, add_ref, one_ref, two_ref, dl_ref):
    lane = iota((8, 128), 1)
    target = jnp.concatenate([meta_ref[16 + r : 17 + r, :] for r in range(8)], axis=1)
    elem_hot = jnp.where((target >> 9) == iota((128, 1024), 0), 1.0, 0.0).astype(BF16)
    for c in range(3):
        value = (TAU / H_STIFF) * value_ref[c : c + 1, :]
        high, low = split2(jnp.broadcast_to(value, (16, 1024)))
        high = elem_hot * jnp.concatenate([high] * 8, axis=0)
        low = elem_hot * jnp.concatenate([low] * 8, axis=0)
        both = jnp.concatenate([high, low], axis=0)
        out = lax.dot_general(node_ref[...], both, NT, preferred_element_type=F32)
        add_ref[c] = (out[:, :128] + out[:, 128:]).reshape(8, 8, 8, 128)
    for y in range(8):
        dl_ref[0, y] = local_diag(c_ref, 0, y)
        dl_ref[1, y] = local_diag(c_ref, 7, y)
        for z in range(1, 7):
            for c in range(3):
                one_ref[c, z, y] = w_ref[z, y] * add_ref[c, z, y]
        for c in range(3):
            s7, s0 = couple(add_ref[c, 7, y], add_ref[c, 0, y], lane)
            one_ref[c, 0, y] = w_ref[0, y] * s0
            one_ref[c, 7, y] = w_ref[7, y] * s7

    def rhs(c, z, y):
        return add_ref[c, z, y]

    coefs = (c_ref, w_ref, dl_ref, rhs)
    one_pass(*coefs, one_ref, two_ref)
    one_pass(*coefs, two_ref, one_ref)
    one_pass(*coefs, one_ref, out_ref, base_ref)


def edge_kernel(
    main_ref, own_ref, below_ref, above_ref, low_ref, high_ref, add_below_ref, add_above_ref, out_ref
):
    lane = iota((8, 128), 1)
    sub = iota((8, 128), 0)
    even, joined = edge_masks()
    y_of = (lane >> 1) & 7
    v = edge_stack(own_ref, below_ref, above_ref, 0, even)
    k = [H_STIFF * c for c in edge_stack(own_ref, below_ref, above_ref, 64, even)]
    rhs = [H_MASS * v[i] for i in range(16)]
    for z in range(8):
        part, rows = (low_ref, high_ref)[z // 4], slice(z % 4 * 8, z % 4 * 8 + 8)
        mine = part[rows, :]
        lower, upper = jnp.where(even, mine, 0.0), jnp.where(even, 0.0, mine)
        if z >= 4:
            lower = jnp.where(even, mine, pltpu.roll(add_below_ref[rows, :], 1, 1))
        else:
            upper = jnp.where(even, pltpu.roll(add_above_ref[rows, :], 127, 1), mine)
        rhs[z] = rhs[z] + lower
        rhs[8 + z] = rhs[8 + z] + upper
    ky = [jnp.where(y_of < 7, k[i], 0.0) for i in range(16)]
    kx = [jnp.where(sub < 7, k[i], 0.0) for i in range(16)]
    diag = []
    for i in range(16):
        d = H_MASS + kx[i] + pltpu.roll(kx[i], 1, 0) + ky[i] + pltpu.roll(ky[i], 2, 1)
        if i % 8 < 7:
            d = d + k[i]
        if i % 8 > 0:
            d = d + k[i - 1]
        diag.append(d)
    d7, d8 = diag[7], diag[8]
    diag[7], diag[8] = d7 + jnp.where(joined, d8, 0.0), d8 + jnp.where(joined, d7, 0.0)
    w = [OMEGA / d for d in diag]
    now = v
    for number in range(NPASS):
        now = edge_pass(number, now, rhs, k, ky, kx, w, d7, d8, joined)
    for c in range(3):
        for y in range(8):
            back = (127 - 2 * (c * 8 + y)) % 128
            for z in range(8):
                new = now[z] if z >= 4 else now[8 + z]
                where = lane == (127 if z >= 4 else 0)
                out_ref[c, z, y] = jnp.where(where, pltpu.roll(new, back, 1), main_ref[c, z, y])


def exchange(rows, count):
    chunks = rows.reshape(PEERS, count, 1, 128)
    return lax.all_to_all(chunks, "sess", 0, 0, tiled=True).reshape(PEERS * count, 128)


def call(kernel, outs, args, scratch=(), limit=24, space=pltpu.VMEM, cost=None):
    single = len(outs) == 1
    spec = pl.BlockSpec(memory_space=pltpu.VMEM)
    return pl.pallas_call(
        kernel,
        out_shape=outs[0] if single else outs,
        in_specs=[pl.BlockSpec(memory_space=space)] * len(args),
        out_specs=spec if single else [spec] * len(outs),
        scratch_shapes=list(scratch),
        compiler_params=pltpu.CompilerParams(vmem_limit_bytes=limit * 1024 * 1024),
        cost_estimate=cost,
    )(*args)


def sds(*shape, dtype=F32):
    return jax.ShapeDtypeStruct(shape, dtype)


def body(velocity_old, conductance, donor_rank, donor_elem, target_node, iface_weights):
    rank = donor_rank.reshape(8, 128)
    elem = donor_elem.reshape(8, 128)
    target = target_node.reshape(8, 128)
    weights = iface_weights.reshape(24, 1024)
    send, meta = call(
        pack_kernel,
        [sds(PEERS * 25, 128), sds(24, 128, dtype=I32)],
        [rank, elem, weights, target],
        [
            pltpu.VMEM((8, 128), I32),
            pltpu.VMEM((8, 128), I32),
            pltpu.VMEM((24, 1024), F32),
            pltpu.VMEM((8, 128), I32),
            pltpu.VMEM((PEERS, 128), I32),
            pltpu.VMEM((PEERS, 128), I32),
            pltpu.SemaphoreType.DMA((4,)),
        ],
        space=pl.ANY,
        limit=56,
    )
    up = [(i, (i + 1) % BLOCKS) for i in range(BLOCKS)]
    down = [(j, i) for i, j in up]
    recv = exchange(send, 25)
    plane = (8, 8, 8, 128)
    own, split, first = call(
        ends_kernel,
        [sds(128, 128), sds(1024, 256, dtype=BF16), sds(*plane)],
        [velocity_old, conductance],
    )
    below = lax.ppermute(own, "blk", up)
    above = lax.ppermute(own, "blk", down)
    base, w, nodes = call(
        base_kernel,
        [sds(3, *plane), sds(*plane), sds(512, 1024, dtype=BF16)],
        [velocity_old, conductance, meta],
        [pltpu.VMEM((3,) + plane, F32), pltpu.VMEM((2, 8, 8, 128), F32)],
        cost=pl.CostEstimate(flops=20_000_000, bytes_accessed=6_000_000, transcendentals=0),
    )
    recv, below, above, base, w, nodes = lax.optimization_barrier(
        (recv, below, above, base, w, nodes)
    )
    reply = call(serve_kernel, [sds(PEERS * 3, 128)], [recv, split, first])
    reply = exchange(reply, 3)
    iface_values, values, add_low, add_high = call(
        finish_kernel, [sds(3, 1024), sds(3, 1024), sds(32, 128), sds(32, 128)], [reply, meta]
    )
    add_below = lax.ppermute(add_high, "blk", up)
    add_above = lax.ppermute(add_low, "blk", down)
    main = call(
        main_kernel,
        [sds(3, *plane)],
        [values, meta, nodes, base, w, conductance],
        [pltpu.VMEM((3,) + plane, F32)] * 3 + [pltpu.VMEM((2, 8, 8, 128), F32)],
        cost=pl.CostEstimate(flops=20_000_000, bytes_accessed=6_000_000, transcendentals=0),
    )
    field = call(
        edge_kernel, [sds(3, *plane)], [main, own, below, above, add_low, add_high, add_below, add_above]
    )
    return field, iface_values


def solution(mesh):
    in_specs = (
        P(None, None, None, None, ("sess", "blk")),
        P(None, None, None, ("sess", "blk")),
        P(("sess", "blk")),
        P(("sess", "blk")),
        P(("sess", "blk")),
        P(None, None, ("sess", "blk")),
    )
    out_specs = (P(None, None, None, None, ("sess", "blk")), P(None, ("sess", "blk")))
    return jax.shard_map(body, mesh=mesh, in_specs=in_specs, out_specs=out_specs, check_vma=False)
```

time: 56.6 us -> 52 us (0.919)
  blocking collectives: 20.8 us -> 17.1 us
  starting transfers between devices: 18 us -> 15.9 us
  local copies, waits for them, and re-layouts: 3.07 us -> 4.21 us
  Pallas kernels: 12.3 us -> 11.7 us
    ppermute x2, starting transfers between devices: 5.58 us -> 1.47 us  [the longest x1 0.87 us: body(): add_below = lax.ppermute(add_high, 'blk', up)]
    all_to_all x1, blocking collectives: 20.8 us -> 17.1 us  [exchange(): lax.all_to_all(chunks, 'sess', 0, 0, tiled=True).reshape(PEERS * count, 128)]
    all_to_all x1, starting transfers between devices: 6.73 us -> 8.82 us  [exchange(): lax.all_to_all(chunks, 'sess', 0, 0, tiled=True).reshape(PEERS * count, 128)]
    all_to_all x1, waiting for transfers between devices: 1.25 us -> 0.01 us  [exchange(): lax.all_to_all(chunks, 'sess', 0, 0, tiled=True).reshape(PEERS * count, 128)]
    ppermute x1, waiting for transfers between devices: 0.01 us -> 1.21 us  [body(): below = lax.ppermute(own, 'blk', up)]
    unnamed x16 -> x30, local copies, waits for them, and re-layouts: 3.07 us -> 4.21 us
    pallas_call x6 -> x7, Pallas kernels: 12.3 us -> 11.7 us  [call(): pl.pallas_call(kernel, out_shape=outs[0] if single else outs, in_specs=[p...]
where the time goes in v1:
time: 52 us; the launch traced here: 51.7 us
  blocking collectives  17.1 us (33%)
  starting transfers between devices  15.9 us (31%)
  Pallas kernels  11.7 us (22%)
  local copies, waits for them, and re-layouts  4.21 us (8%)
  waiting for transfers between devices  1.96 us (4%)
  between operations  0.79 us (2%)
    all_to_all x1, blocking collectives, exchange(): lax.all_to_all(chunks, 'sess', 0, 0, tiled=True).reshape(PEERS * count, 128)  17.1 us
    pallas_call x7, Pallas kernels, call(): pl.pallas_call(kernel, out_shape=outs[0] if single else outs, in_specs=[p...  11.7 us
    all_to_all x1, starting transfers between devices, exchange(): lax.all_to_all(chunks, 'sess', 0, 0, tiled=True).reshape(PEERS * count, 128)  8.82 us
    ppermute x1, starting transfers between devices, body(): above = lax.ppermute(own, 'blk', down)  5.65 us
    unnamed x30, local copies, waits for them, and re-layouts  4.21 us
    ppermute x1, waiting for transfers between devices, body(): below = lax.ppermute(own, 'blk', up)  1.21 us
  transfers between devices with their start and end apart: 5, of which 2 were waited for; matrix products, arithmetic and copies ran while one was open for 0% of the time, Pallas kernels for 10%

profile of v1, /device:TPU:1, one launch (start us, length us, event | category | flops | bytes accessed | tf_op | source)
XLA Modules:
  0.0 51.7 jit_solution(18189046215210418485)
XLA Ops:
  0.6 2.4 %shard_map.77 = (f32[800,128]{1,0:T(8,128)}, s32[24,128]{1,0:T(8,128)}) custom-call(s32[8,128]{1,0:T(8,128)} %bitcast.13, s32[8,128]{1,0:T(8,128)} %bitcast.14, f32[24,1024]{1,0:T(8,128)} %bitcast.12, s32[8,128]{1,0:T(8,128)} %bitcast.15), custom_call_target="tpu_custom_call" | custom-call | tf_op jit(solution)/shard_map/pallas_call | solution.py:401
  3.0 8.8 %all-to-all-start = ((f32[32,25,1,128]{3,2,1,0:T(1,128)}), f32[32,25,1,128]{3,2,1,0:T(1,128)S(1)}, u32[]{:S(2)}, u32[]{:S(2)}) async-start(f32[32,25,1,128]{3,2,1,0:T(1,128)} %bitcast.11), calls=%async_computation | async-start | bytes 819200 | tf_op jit(solution)/shard_map/all_to_all | solution.py:395
  11.8 0.0 copy-start.1
  11.9 0.9 %copy-done.1 = f32[8,8,8,128]{3,2,1,0:T(8,128)S(1)} copy-done((f32[8,8,8,128]{3,2,1,0:T(8,128)S(1)}, f32[8,8,8,128]{3,2,1,0:T(8,128)}, u32[]{:S(2)}) %copy-start.1) | copy-done | bytes 262168
  12.8 0.8 %shard_map.78 = (f32[128,128]{1,0:T(8,128)S(1)}, bf16[1024,256]{1,0:T(8,128)(2,1)S(1)}, f32[8,8,8,128]{3,2,1,0:T(8,128)S(1)}) custom-call(f32[3,8,8,8,128]{4,3,2,1,0:T(8,128)S(1)} %copy-done, f32[8,8,8,128]{3,2,1,0:T(8,128)S(1)} %copy-done.1), custom_call_target="tpu_custom_call" | custom-call | tf_op jit(solution)/shard_map/pallas_call | solution.py:401
  13.6 0.0 copy-start.3
  13.6 5.7 %collective-permute-start.1 = (f32[128,128]{1,0:T(8,128)S(1)}, f32[128,128]{1,0:T(8,128)S(1)}, u32[]{:S(2)}, u32[]{:S(2)}) collective-permute-start(f32[128,128]{1,0:T(8,128)S(1)} %get-tuple-element.21.own_ref), channel_id=1, source_target_pairs={{1,0},{2,1},{3,2},{4,3},{5,4},{6,5},{7,6},{0,7},{9,8},{10,9},{11,1... | collective-permute-start | bytes 196616 | tf_op jit(solution)/shard_map/ppermute | solution.py:447
  19.3 0.0 collective-permute-start
  19.3 2.4 %shard_map.79 = (f32[3,8,8,8,128]{4,3,2,1,0:T(8,128)S(1)}, f32[8,8,8,128]{3,2,1,0:T(8,128)S(1)}, bf16[512,1024]{1,0:T(8,128)(2,1)S(1)}) custom-call(f32[3,8,8,8,128]{4,3,2,1,0:T(8,128)S(1)} %copy-done, f32[8,8,8,128]{3,2,1,0:T(8,128)S(1)} %copy-done.2, s32[24,128]{1,0:T(8,128)S(1)} %copy-done.7), custom_call_target="tpu_custom_call" | custom-call | flops 20000000 | bytes 6000000 | tf_op jit(solution)/shard_map/pallas_call | solution.py:401
  21.7 0.0 collective-permute-done.1.above_ref
  21.8 0.6 %copy-done.11 = f32[128,128]{1,0:T(8,128)} copy-done((f32[128,128]{1,0:T(8,128)}, f32[128,128]{1,0:T(8,128)S(1)}, u32[]{:S(2)}) %copy-start.11) | copy-done | bytes 65560
  22.4 1.2 %collective-permute-done.below_ref = f32[128,128]{1,0:T(8,128)S(1)} collective-permute-done((f32[128,128]{1,0:T(8,128)S(1)}, f32[128,128]{1,0:T(8,128)S(1)}, u32[]{:S(2)}, u32[]{:S(2)}) %collective-permute-start) | collective-permute-done | bytes 65568 | tf_op jit(solution)/shard_map/ppermute | solution.py:446
  23.6 0.6 %copy-done.13 = f32[128,128]{1,0:T(8,128)} copy-done((f32[128,128]{1,0:T(8,128)}, f32[128,128]{1,0:T(8,128)S(1)}, u32[]{:S(2)}) %copy-start.13) | copy-done | bytes 65560
  24.2 1.0 %copy-done.4 = bf16[1024,256]{1,0:T(8,128)(2,1)S(1)} copy-done((bf16[1024,256]{1,0:T(8,128)(2,1)S(1)}, bf16[1024,256]{1,0:T(8,128)(2,1)}, u32[]{:S(2)}) %copy-start.4) | copy-done | bytes 524312
  25.3 0.9 %copy-done.6 = f32[8,8,8,128]{3,2,1,0:T(8,128)S(1)} copy-done((f32[8,8,8,128]{3,2,1,0:T(8,128)S(1)}, f32[8,8,8,128]{3,2,1,0:T(8,128)}, u32[]{:S(2)}) %copy-start.6) | copy-done | bytes 262168
  26.2 1.4 %shard_map.80 = f32[96,128]{1,0:T(8,128)S(1)} custom-call(f32[800,128]{1,0:T(8,128)S(1)} %bitcast.8, bf16[1024,256]{1,0:T(8,128)(2,1)S(1)} %copy-done.4, f32[8,8,8,128]{3,2,1,0:T(8,128)S(1)} %copy-done.6), custom_call_target="tpu_custom_call" | custom-call | tf_op jit(solution)/shard_map/pallas_call | solution.py:401
  27.6 0.0 copy-start.8
  27.7 17.1 %all_to_all.10 = f32[32,3,1,128]{3,2,1,0:T(1,128)S(1)} all-to-all(f32[32,3,1,128]{3,2,1,0:T(1,128)S(1)} %bitcast.9), channel_id=1, replica_groups=mesh['sess'=32,'blk'=8] {'sess'}, dimensions={0} | all-to-all | bytes 98304 | tf_op jit(solution)/shard_map/all_to_all | solution.py:395
  44.8 0.9 %shard_map.81 = (f32[3,1024]{1,0:T(4,128)}, f32[3,1024]{1,0:T(4,128)S(1)}, f32[32,128]{1,0:T(8,128)S(1)}, f32[32,128]{1,0:T(8,128)S(1)}) custom-call(f32[96,128]{1,0:T(8,128)S(1)} %bitcast.10, s32[24,128]{1,0:T(8,128)S(1)} %copy-done.8), custom_call_target="tpu_custom_call" | custom-call | tf_op jit(solution)/shard_map/pallas_call | solution.py:401
  45.7 0.6 %collective-permute-start.3 = (f32[32,128]{1,0:T(8,128)S(1)}, f32[32,128]{1,0:T(8,128)S(1)}, u32[]{:S(2)}, u32[]{:S(2)}) collective-permute-start(f32[32,128]{1,0:T(8,128)S(1)} %get-tuple-element.35.low_ref), channel_id=1, source_target_pairs={{1,0},{2,1},{3,2},{4,3},{5,4},{6,5},{7,6},{0,7},{9,8},{10,9},{11,1... | collective-permute-start | bytes 49160 | tf_op jit(solution)/shard_map/ppermute | solution.py:464
  46.3 0.9 %collective-permute-start.2 = (f32[32,128]{1,0:T(8,128)S(1)}, f32[32,128]{1,0:T(8,128)S(1)}, u32[]{:S(2)}, u32[]{:S(2)}) collective-permute-start(f32[32,128]{1,0:T(8,128)S(1)} %get-tuple-element.36.high_ref), channel_id=1, source_target_pairs={{0,1},{1,2},{2,3},{3,4},{4,5},{5,6},{6,7},{7,0},{8,9},{9,10},{10,1... | collective-permute-start | bytes 49160 | tf_op jit(solution)/shard_map/ppermute | solution.py:463
  47.2 2.2 %shard_map.82.main_ref = f32[3,8,8,8,128]{4,3,2,1,0:T(8,128)S(1)} custom-call(f32[3,1024]{1,0:T(4,128)S(1)} %get-tuple-element.29.value_ref, s32[24,128]{1,0:T(8,128)S(1)} %copy-done.8, bf16[512,1024]{1,0:T(8,128)(2,1)S(1)} %get-tuple-element.30.node_ref, f32[3,8,8,8,128]{4,3,2,1,0:T(8,128)S(1)} %get-tuple-element.31.base_ref, ...), custom_call_target="tpu_custom_call" | custom-call | flops 20000000 | bytes 6000000 | tf_op jit(solution)/shard_map/pallas_call | solution.py:401
  49.3 0.7 %collective-permute-done.2.add_below_ref = f32[32,128]{1,0:T(8,128)S(1)} collective-permute-done((f32[32,128]{1,0:T(8,128)S(1)}, f32[32,128]{1,0:T(8,128)S(1)}, u32[]{:S(2)}, u32[]{:S(2)}) %collective-permute-start.2) | collective-permute-done | bytes 16416 | tf_op jit(solution)/shard_map/ppermute | solution.py:463
  50.1 1.6 %shard_map.83 = f32[3,8,8,8,128]{4,3,2,1,0:T(8,128)} custom-call(f32[3,8,8,8,128]{4,3,2,1,0:T(8,128)S(1)} %shard_map.82.main_ref, f32[128,128]{1,0:T(8,128)S(1)} %copy-done.10, f32[128,128]{1,0:T(8,128)S(1)} %copy-done.14, f32[128,128]{1,0:T(8,128)S(1)} %copy-done.12, f32[32,128]{1,0:T(8,128)S(1)} %get-tuple-element.35.low_ref, ...), custom_call_target="tpu_custom_call" | custom-call | tf_op jit(solution)/shard_map/pallas_call | solution.py:401
  (24 shorter events, 0.0 us)
Async XLA Ops:
  0.6 11.2 %copy-start = (f32[3,8,8,8,128]{4,3,2,1,0:T(8,128)S(1)}, f32[3,8,8,8,128]{4,3,2,1,0:T(8,128)}, u32[]{:S(2)}) copy-start(f32[3,8,8,8,128]{4,3,2,1,0:T(8,128)} %v_ref.3) | copy-start | bytes 2359300
  3.0 21.2 %all-to-all-start = ((f32[32,25,1,128]{3,2,1,0:T(1,128)}), f32[32,25,1,128]{3,2,1,0:T(1,128)S(1)}, u32[]{:S(2)}, u32[]{:S(2)}) async-start(f32[32,25,1,128]{3,2,1,0:T(1,128)} %bitcast.11), calls=%async_computation | async-start | bytes 819200 | tf_op jit(solution)/shard_map/all_to_all | solution.py:395
  11.8 1.0 %copy-start.1 = (f32[8,8,8,128]{3,2,1,0:T(8,128)S(1)}, f32[8,8,8,128]{3,2,1,0:T(8,128)}, u32[]{:S(2)}) copy-start(f32[8,8,8,128]{3,2,1,0:T(8,128)} %c_ref.5) | copy-start | bytes 786436
  12.8 6.5 %copy-start.2 = (f32[8,8,8,128]{3,2,1,0:T(8,128)S(1)}, f32[8,8,8,128]{3,2,1,0:T(8,128)}, u32[]{:S(2)}) copy-start(f32[8,8,8,128]{3,2,1,0:T(8,128)} %c_ref.5) | copy-start | bytes 786436
  12.8 6.5 %copy-start.7 = (s32[24,128]{1,0:T(8,128)S(1)}, s32[24,128]{1,0:T(8,128)}, u32[]{:S(2)}) copy-start(s32[24,128]{1,0:T(8,128)} %get-tuple-element.22.meta_ref) | copy-start | bytes 36868
  13.6 8.1 %copy-start.3 = (bf16[1024,256]{1,0:T(8,128)(2,1)}, bf16[1024,256]{1,0:T(8,128)(2,1)S(1)}, u32[]{:S(2)}) copy-start(bf16[1024,256]{1,0:T(8,128)(2,1)S(1)} %get-tuple-element.27.split_ref) | copy-start | bytes 1572868
  13.6 8.1 %copy-start.5 = (f32[8,8,8,128]{3,2,1,0:T(8,128)}, f32[8,8,8,128]{3,2,1,0:T(8,128)S(1)}, u32[]{:S(2)}) copy-start(f32[8,8,8,128]{3,2,1,0:T(8,128)S(1)} %get-tuple-element.28.first_ref) | copy-start | bytes 786436
  13.6 8.1 %copy-start.9 = (f32[128,128]{1,0:T(8,128)}, f32[128,128]{1,0:T(8,128)S(1)}, u32[]{:S(2)}) copy-start(f32[128,128]{1,0:T(8,128)S(1)} %get-tuple-element.21.own_ref) | copy-start | bytes 196612
  13.6 8.1 %collective-permute-start.1 = (f32[128,128]{1,0:T(8,128)S(1)}, f32[128,128]{1,0:T(8,128)S(1)}, u32[]{:S(2)}, u32[]{:S(2)}) collective-permute-start(f32[128,128]{1,0:T(8,128)S(1)} %get-tuple-element.21.own_ref), channel_id=1, source_target_pairs={{1,0},{2,1},{3,2},{4,3},{5,4},{6,5},{7,6},{0,7},{9,8},{10,9},{11,1... | collective-permute-start | bytes 196616 | tf_op jit(solution)/shard_map/ppermute | solution.py:447
  19.3 4.3 %collective-permute-start = (f32[128,128]{1,0:T(8,128)S(1)}, f32[128,128]{1,0:T(8,128)S(1)}, u32[]{:S(2)}, u32[]{:S(2)}) collective-permute-start(f32[128,128]{1,0:T(8,128)S(1)} %get-tuple-element.21.own_ref), channel_id=1, source_target_pairs={{0,1},{1,2},{2,3},{3,4},{4,5},{5,6},{6,7},{7,0},{8,9},{9,10},{10,1... | collective-permute-start | bytes 196616 | tf_op jit(solution)/shard_map/ppermute | solution.py:446
  21.8 0.6 %copy-start.11 = (f32[128,128]{1,0:T(8,128)}, f32[128,128]{1,0:T(8,128)S(1)}, u32[]{:S(2)}) copy-start(f32[128,128]{1,0:T(8,128)S(1)} %collective-permute-done.1.above_ref) | copy-start | bytes 196612
  23.6 0.6 %copy-start.13 = (f32[128,128]{1,0:T(8,128)}, f32[128,128]{1,0:T(8,128)S(1)}, u32[]{:S(2)}) copy-start(f32[128,128]{1,0:T(8,128)S(1)} %collective-permute-done.below_ref) | copy-start | bytes 196612
  24.2 1.0 %copy-start.4 = (bf16[1024,256]{1,0:T(8,128)(2,1)S(1)}, bf16[1024,256]{1,0:T(8,128)(2,1)}, u32[]{:S(2)}) copy-start(bf16[1024,256]{1,0:T(8,128)(2,1)} %copy-done.3) | copy-start | bytes 1572868
  25.3 0.9 %copy-start.6 = (f32[8,8,8,128]{3,2,1,0:T(8,128)S(1)}, f32[8,8,8,128]{3,2,1,0:T(8,128)}, u32[]{:S(2)}) copy-start(f32[8,8,8,128]{3,2,1,0:T(8,128)} %copy-done.5) | copy-start | bytes 786436
  27.6 17.1 %copy-start.8 = (s32[24,128]{1,0:T(8,128)S(1)}, s32[24,128]{1,0:T(8,128)}, u32[]{:S(2)}) copy-start(s32[24,128]{1,0:T(8,128)} %get-tuple-element.22.meta_ref) | copy-start | bytes 36868
  45.7 3.6 %collective-permute-start.3 = (f32[32,128]{1,0:T(8,128)S(1)}, f32[32,128]{1,0:T(8,128)S(1)}, u32[]{:S(2)}, u32[]{:S(2)}) collective-permute-start(f32[32,128]{1,0:T(8,128)S(1)} %get-tuple-element.35.low_ref), channel_id=1, source_target_pairs={{1,0},{2,1},{3,2},{4,3},{5,4},{6,5},{7,6},{0,7},{9,8},{10,9},{11,1... | collective-permute-start | bytes 49160 | tf_op jit(solution)/shard_map/ppermute | solution.py:464
  46.3 3.8 %collective-permute-start.2 = (f32[32,128]{1,0:T(8,128)S(1)}, f32[32,128]{1,0:T(8,128)S(1)}, u32[]{:S(2)}, u32[]{:S(2)}) collective-permute-start(f32[32,128]{1,0:T(8,128)S(1)} %get-tuple-element.36.high_ref), channel_id=1, source_target_pairs={{0,1},{1,2},{2,3},{3,4},{4,5},{5,6},{6,7},{7,0},{8,9},{9,10},{10,1... | collective-permute-start | bytes 49160 | tf_op jit(solution)/shard_map/ppermute | solution.py:463
  47.2 2.9 %copy-start.10 = (f32[128,128]{1,0:T(8,128)S(1)}, f32[128,128]{1,0:T(8,128)}, u32[]{:S(2)}) copy-start(f32[128,128]{1,0:T(8,128)} %copy-done.9) | copy-start | bytes 196612
  47.2 2.9 %copy-start.12 = (f32[128,128]{1,0:T(8,128)S(1)}, f32[128,128]{1,0:T(8,128)}, u32[]{:S(2)}) copy-start(f32[128,128]{1,0:T(8,128)} %copy-done.11) | copy-start | bytes 196612
  47.2 2.9 %copy-start.14 = (f32[128,128]{1,0:T(8,128)S(1)}, f32[128,128]{1,0:T(8,128)}, u32[]{:S(2)}) copy-start(f32[128,128]{1,0:T(8,128)} %copy-done.13) | copy-start | bytes 196612

commit v2 on v1

--- a/solution.py
+++ b/solution.py
@@ -100,12 +100,12 @@
 
 def serve_kernel(recv_ref, split_ref, first_ref, reply_ref):
     outer = lax.axis_index("sess") < BACKGROUND
-    first = jnp.where(outer, BACKGROUND - 1, 0)
-    turns = jnp.where(outer, 3, 6)
+    first = jnp.where(outer, PEERS - 14, 0)
+    turns = jnp.where(outer, 2, 3)
     elem_iota = iota((128, 128), 0)
 
-    def four_peers(turn, carry):
-        peers = [first + turn * 4 + i for i in range(4)]
+    def seven_peers(turn, carry):
+        peers = [first + turn * 7 + i for i in range(7)]
         hot, picks = [], []
         for peer in peers:
             index = recv_ref[pl.ds(peer * 25 + 24, 1), :].astype(I32)
@@ -120,7 +120,7 @@
         for c in range(3):
             if c:
                 rows = slice(c * 512 - 512, c * 512)
-                picked = jnp.dot(split_ref[rows, :], hot, preferred_element_type=F32).reshape(8, 8, 8, 512)
+                picked = jnp.dot(split_ref[rows, :], hot, preferred_element_type=F32).reshape(8, 8, 8, 896)
             for i, peer in enumerate(peers):
                 total = None
                 for z in range(8):
@@ -138,7 +138,7 @@
                 reply_ref[pl.ds(peer * 3 + c, 1), :] = jnp.sum(total * wx, axis=0, keepdims=True)
         return carry
 
-    lax.fori_loop(0, turns, four_peers, 0)
+    lax.fori_loop(0, turns, seven_peers, 0)
 
 
 def finish_kernel(reply_ref, meta_ref, value_ref, copy_ref, low_ref, high_ref):
@@ -346,7 +346,7 @@
 
 
 def edge_kernel(
-    main_ref, own_ref, below_ref, above_ref, low_ref, high_ref, add_below_ref, add_above_ref, out_ref
+    main_ref, own_ref, below_ref, above_ref, low_ref, high_ref, add_below_ref, add_above_ref, out_hbm, out_ref, sems
 ):
     lane = iota((8, 128), 1)
     sub = iota((8, 128), 0)
@@ -381,13 +381,24 @@
     now = v
     for number in range(NPASS):
         now = edge_pass(number, now, rhs, k, ky, kx, w, d7, d8, joined)
+    copies = []
     for c in range(3):
-        for y in range(8):
-            back = (127 - 2 * (c * 8 + y)) % 128
-            for z in range(8):
-                new = now[z] if z >= 4 else now[8 + z]
-                where = lane == (127 if z >= 4 else 0)
-                out_ref[c, z, y] = jnp.where(where, pltpu.roll(new, back, 1), main_ref[c, z, y])
+        for half in range(2):
+            planes = slice(half * 4, half * 4 + 4)
+            for y in range(8):
+                back = (127 - 2 * (c * 8 + y)) % 128
+                where = lane == (0, 127)[half]
+                for z in range(half * 4, half * 4 + 4):
+                    new = pltpu.roll(now[z] if half else now[8 + z], back, 1)
+                    out_ref[c, z, y] = jnp.where(where, new, main_ref[c, z, y])
+            copies.append(
+                pltpu.make_async_copy(
+                    out_ref.at[c, planes], out_hbm.at[c, planes], sems.at[2 * c + half]
+                )
+            )
+            copies[-1].start()
+    for copy in copies:
+        copy.wait()
 
 
 def exchange(rows, count):
@@ -395,9 +406,9 @@
     return lax.all_to_all(chunks, "sess", 0, 0, tiled=True).reshape(PEERS * count, 128)
 
 
-def call(kernel, outs, args, scratch=(), limit=24, space=pltpu.VMEM, cost=None):
+def call(kernel, outs, args, scratch=(), limit=24, space=pltpu.VMEM, out_space=pltpu.VMEM):
     single = len(outs) == 1
-    spec = pl.BlockSpec(memory_space=pltpu.VMEM)
+    spec = pl.BlockSpec(memory_space=out_space)
     return pl.pallas_call(
         kernel,
         out_shape=outs[0] if single else outs,
@@ -405,7 +416,6 @@
         out_specs=spec if single else [spec] * len(outs),
         scratch_shapes=list(scratch),
         compiler_params=pltpu.CompilerParams(vmem_limit_bytes=limit * 1024 * 1024),
-        cost_estimate=cost,
     )(*args)
 
 
@@ -445,18 +455,17 @@
     )
     below = lax.ppermute(own, "blk", up)
     above = lax.ppermute(own, "blk", down)
+    recv, below, above = lax.optimization_barrier((recv, below, above))
+    reply = call(serve_kernel, [sds(PEERS * 3, 128)], [recv, split, first])
+    reply, v_later, c_later = lax.optimization_barrier((reply, velocity_old, conductance))
+    reply = exchange(reply, 3)
     base, w, nodes = call(
         base_kernel,
         [sds(3, *plane), sds(*plane), sds(512, 1024, dtype=BF16)],
-        [velocity_old, conductance, meta],
+        [v_later, c_later, meta],
         [pltpu.VMEM((3,) + plane, F32), pltpu.VMEM((2, 8, 8, 128), F32)],
-        cost=pl.CostEstimate(flops=20_000_000, bytes_accessed=6_000_000, transcendentals=0),
-    )
-    recv, below, above, base, w, nodes = lax.optimization_barrier(
-        (recv, below, above, base, w, nodes)
-    )
-    reply = call(serve_kernel, [sds(PEERS * 3, 128)], [recv, split, first])
-    reply = exchange(reply, 3)
+    )
+    reply, base, w, nodes = lax.optimization_barrier((reply, base, w, nodes))
     iface_values, values, add_low, add_high = call(
         finish_kernel, [sds(3, 1024), sds(3, 1024), sds(32, 128), sds(32, 128)], [reply, meta]
     )
@@ -465,12 +474,15 @@
     main = call(
         main_kernel,
         [sds(3, *plane)],
-        [values, meta, nodes, base, w, conductance],
+        [values, meta, nodes, base, w, c_later],
         [pltpu.VMEM((3,) + plane, F32)] * 3 + [pltpu.VMEM((2, 8, 8, 128), F32)],
-        cost=pl.CostEstimate(flops=20_000_000, bytes_accessed=6_000_000, transcendentals=0),
     )
     field = call(
-        edge_kernel, [sds(3, *plane)], [main, own, below, above, add_low, add_high, add_below, add_above]
+        edge_kernel,
+        [sds(3, *plane)],
+        [main, own, below, above, add_low, add_high, add_below, add_above],
+        [pltpu.VMEM((3,) + plane, F32), pltpu.SemaphoreType.DMA((6,))],
+        out_space=pl.ANY,
     )
     return field, iface_values
 

time: 52 us -> 49.1 us (0.944)
  blocking collectives: 17.1 us -> 0 us
  starting transfers between devices: 15.9 us -> 25.4 us
  waiting for transfers between devices: 1.96 us -> 9.12 us
  local copies, waits for them, and re-layouts: 4.21 us -> 0.96 us
  Pallas kernels: 11.7 us -> 12.6 us
    all_to_all x1 -> x0, blocking collectives: 17.1 us -> none  [exchange(): lax.all_to_all(chunks, 'sess', 0, 0, tiled=True).reshape(PEERS * count, 128)]
    all_to_all x1 -> x2, starting transfers between devices: 8.82 us -> 18.3 us  [exchange(): lax.all_to_all(chunks, 'sess', 0, 0, tiled=True).reshape(PEERS * count, 128)]
    all_to_all x1 -> x2, waiting for transfers between devices: 0.01 us -> 4.73 us  [exchange(): lax.all_to_all(chunks, 'sess', 0, 0, tiled=True).reshape(PEERS * count, 128)]
    unnamed x30 -> x8, local copies, waits for them, and re-layouts: 4.21 us -> 0.96 us
    ppermute x1, waiting for transfers between devices: 1.21 us -> 2.99 us  [body(): below = lax.ppermute(own, 'blk', up)]
    ppermute x1, waiting for transfers between devices: 0.01 us -> 1.33 us  [body(): above = lax.ppermute(own, 'blk', down)]
    pallas_call x7, Pallas kernels: 11.7 us -> 12.6 us  [call(): pl.pallas_call(kernel, out_shape=outs[0] if single else outs, in_specs=[p...]
    ppermute x1, waiting for transfers between devices: 0.74 us -> 0.06 us  [body(): add_below = lax.ppermute(add_high, 'blk', up)]
  transfers between devices with their start and end apart: 5 -> 6, of which waited for: 2 -> 4; matrix products, arithmetic and copies ran while one was open for 0% -> 0% of each run, Pallas kernels for 10% -> 11%
where the time goes in v2:
time: 49.1 us; the launch traced here: 48.8 us
  starting transfers between devices  25.4 us (52%)
  Pallas kernels  12.6 us (26%)
  waiting for transfers between devices  9.12 us (19%)
  local copies, waits for them, and re-layouts  0.96 us (2%)
  between operations  0.72 us (1%)
    all_to_all x2, starting transfers between devices, exchange(): lax.all_to_all(chunks, 'sess', 0, 0, tiled=True).reshape(PEERS * count, 128)  18.3 us
    pallas_call x7, Pallas kernels, call(): pl.pallas_call(kernel, out_shape=outs[0] if single else outs, in_specs=[p...  12.6 us
    ppermute x1, starting transfers between devices, body(): above = lax.ppermute(own, 'blk', down)  5.65 us
    all_to_all x2, waiting for transfers between devices, exchange(): lax.all_to_all(chunks, 'sess', 0, 0, tiled=True).reshape(PEERS * count, 128)  4.73 us
    ppermute x1, waiting for transfers between devices, body(): below = lax.ppermute(own, 'blk', up)  2.99 us
    ppermute x1, starting transfers between devices, body(): add_below = lax.ppermute(add_high, 'blk', up)  1.46 us
    ppermute x1, waiting for transfers between devices, body(): above = lax.ppermute(own, 'blk', down)  1.33 us
  transfers between devices with their start and end apart: 6, of which 4 were waited for; matrix products, arithmetic and copies ran while one was open for 0% of the time, Pallas kernels for 11%

profile of v2, /device:TPU:1, one launch (start us, length us, event | category | flops | bytes accessed | tf_op | source)
XLA Modules:
  0.0 48.8 jit_solution(15473730981849924969)
XLA Ops:
  0.6 2.4 %shard_map.77 = (f32[800,128]{1,0:T(8,128)}, s32[24,128]{1,0:T(8,128)}) custom-call(s32[8,128]{1,0:T(8,128)} %bitcast.12, s32[8,128]{1,0:T(8,128)} %bitcast.13, f32[24,1024]{1,0:T(8,128)} %bitcast.11, s32[8,128]{1,0:T(8,128)} %bitcast.14), custom_call_target="tpu_custom_call" | custom-call | tf_op jit(solution)/shard_map/pallas_call | solution.py:412
  3.0 8.8 %all-to-all-start = ((f32[32,25,1,128]{3,2,1,0:T(1,128)}), f32[32,25,1,128]{3,2,1,0:T(1,128)S(1)}, u32[]{:S(2)}, u32[]{:S(2)}) async-start(f32[32,25,1,128]{3,2,1,0:T(1,128)} %bitcast.10), calls=%async_computation | async-start | bytes 819200 | tf_op jit(solution)/shard_map/all_to_all | solution.py:406
  11.8 0.0 copy-done
  11.8 0.0 copy-start.1
  11.9 0.9 %copy-done.1 = f32[8,8,8,128]{3,2,1,0:T(8,128)S(1)} copy-done((f32[8,8,8,128]{3,2,1,0:T(8,128)S(1)}, f32[8,8,8,128]{3,2,1,0:T(8,128)}, u32[]{:S(2)}) %copy-start.1) | copy-done | bytes 262168
  12.8 0.8 %shard_map.78 = (f32[128,128]{1,0:T(8,128)S(1)}, bf16[1024,256]{1,0:T(8,128)(2,1)S(1)}, f32[8,8,8,128]{3,2,1,0:T(8,128)S(1)}) custom-call(f32[3,8,8,8,128]{4,3,2,1,0:T(8,128)S(1)} %copy-done, f32[8,8,8,128]{3,2,1,0:T(8,128)S(1)} %copy-done.1), custom_call_target="tpu_custom_call" | custom-call | tf_op jit(solution)/shard_map/pallas_call | solution.py:412
  13.6 5.7 %collective-permute-start.1 = (f32[128,128]{1,0:T(8,128)S(1)}, f32[128,128]{1,0:T(8,128)S(1)}, u32[]{:S(2)}, u32[]{:S(2)}) collective-permute-start(f32[128,128]{1,0:T(8,128)S(1)} %get-tuple-element.25.own_ref), channel_id=1, source_target_pairs={{1,0},{2,1},{3,2},{4,3},{5,4},{6,5},{7,6},{0,7},{9,8},{10,9},{11,1... | collective-permute-start | bytes 196616 | tf_op jit(solution)/shard_map/ppermute | solution.py:457
  19.2 0.0 collective-permute-start
  19.2 1.3 %collective-permute-done.1.above_ref = f32[128,128]{1,0:T(8,128)S(1)} collective-permute-done((f32[128,128]{1,0:T(8,128)S(1)}, f32[128,128]{1,0:T(8,128)S(1)}, u32[]{:S(2)}, u32[]{:S(2)}) %collective-permute-start.1) | collective-permute-done | bytes 65568 | tf_op jit(solution)/shard_map/ppermute | solution.py:457
  20.6 3.0 %collective-permute-done.below_ref = f32[128,128]{1,0:T(8,128)S(1)} collective-permute-done((f32[128,128]{1,0:T(8,128)S(1)}, f32[128,128]{1,0:T(8,128)S(1)}, u32[]{:S(2)}, u32[]{:S(2)}) %collective-permute-start) | collective-permute-done | bytes 65568 | tf_op jit(solution)/shard_map/ppermute | solution.py:456
  23.5 0.0 all-to-all-done
  23.6 2.2 %shard_map.79 = f32[96,128]{1,0:T(8,128)} custom-call(f32[800,128]{1,0:T(8,128)S(1)} %bitcast.8, bf16[1024,256]{1,0:T(8,128)(2,1)S(1)} %get-tuple-element.27.split_ref, f32[8,8,8,128]{3,2,1,0:T(8,128)S(1)} %get-tuple-element.28.first_ref), custom_call_target="tpu_custom_call" | custom-call | tf_op jit(solution)/shard_map/pallas_call | solution.py:412
  25.7 9.4 %all-to-all-start.1 = ((f32[32,3,1,128]{3,2,1,0:T(1,128)}), f32[32,3,1,128]{3,2,1,0:T(1,128)S(1)}, u32[]{:S(2)}, u32[]{:S(2)}) async-start(f32[32,3,1,128]{3,2,1,0:T(1,128)} %bitcast.6), calls=%async_computation.1 | async-start | bytes 98304 | tf_op jit(solution)/shard_map/all_to_all | solution.py:406
  35.2 0.0 copy-done.2
  35.2 0.0 copy-done.3
  35.2 2.5 %shard_map.80 = (f32[3,8,8,8,128]{4,3,2,1,0:T(8,128)S(1)}, f32[8,8,8,128]{3,2,1,0:T(8,128)S(1)}, bf16[512,1024]{1,0:T(8,128)(2,1)S(1)}) custom-call(f32[3,8,8,8,128]{4,3,2,1,0:T(8,128)S(1)} %copy-done, f32[8,8,8,128]{3,2,1,0:T(8,128)S(1)} %copy-done.2, s32[24,128]{1,0:T(8,128)S(1)} %copy-done.3), custom_call_target="tpu_custom_call" | custom-call | tf_op jit(solution)/shard_map/pallas_call | solution.py:412
  37.7 4.7 %all-to-all-done.1 = f32[32,3,1,128]{3,2,1,0:T(1,128)S(1)} async-done(((f32[32,3,1,128]{3,2,1,0:T(1,128)}), f32[32,3,1,128]{3,2,1,0:T(1,128)S(1)}, u32[]{:S(2)}, u32[]{:S(2)}) %all-to-all-start.1) | async-done | bytes 49184 | tf_op jit(solution)/shard_map/all_to_all | solution.py:406
  42.5 0.9 %shard_map.81 = (f32[3,1024]{1,0:T(4,128)}, f32[3,1024]{1,0:T(4,128)S(1)}, f32[32,128]{1,0:T(8,128)S(1)}, f32[32,128]{1,0:T(8,128)S(1)}) custom-call(f32[96,128]{1,0:T(8,128)S(1)} %bitcast.9, s32[24,128]{1,0:T(8,128)S(1)} %copy-done.3), custom_call_target="tpu_custom_call" | custom-call | tf_op jit(solution)/shard_map/pallas_call | solution.py:412
  43.4 0.0 collective-permute-start.3
  43.4 1.5 %collective-permute-start.2 = (f32[32,128]{1,0:T(8,128)S(1)}, f32[32,128]{1,0:T(8,128)S(1)}, u32[]{:S(2)}, u32[]{:S(2)}) collective-permute-start(f32[32,128]{1,0:T(8,128)S(1)} %get-tuple-element.44.high_ref), channel_id=1, source_target_pairs={{0,1},{1,2},{2,3},{3,4},{4,5},{5,6},{6,7},{7,0},{8,9},{9,10},{10,1... | collective-permute-start | bytes 49160 | tf_op jit(solution)/shard_map/ppermute | solution.py:472
  44.8 2.3 %shard_map.82.main_ref = f32[3,8,8,8,128]{4,3,2,1,0:T(8,128)S(1)} custom-call(f32[3,1024]{1,0:T(4,128)S(1)} %get-tuple-element.37.value_ref, s32[24,128]{1,0:T(8,128)S(1)} %copy-done.3, bf16[512,1024]{1,0:T(8,128)(2,1)S(1)} %get-tuple-element.38.node_ref, f32[3,8,8,8,128]{4,3,2,1,0:T(8,128)S(1)} %get-tuple-element.39.base_ref, ...), custom_call_target="tpu_custom_call" | custom-call | tf_op jit(solution)/shard_map/pallas_call | solution.py:412
  47.1 0.0 collective-permute-done.3.add_above_ref
  47.1 0.1 collective-permute-done.2.add_below_ref
  47.2 1.6 %shard_map.83 = f32[3,8,8,8,128]{4,3,2,1,0:T(8,128)} custom-call(f32[3,8,8,8,128]{4,3,2,1,0:T(8,128)S(1)} %shard_map.82.main_ref, f32[128,128]{1,0:T(8,128)S(1)} %get-tuple-element.25.own_ref, f32[128,128]{1,0:T(8,128)S(1)} %collective-permute-done.below_ref, f32[128,128]{1,0:T(8,128)S(1)} %collective-permute-done.1.above_ref, ...), custom_call_target="tpu_custom_call" | custom-call | tf_op jit(solution)/shard_map/pallas_call | solution.py:412
  (3 shorter events, 0.0 us)
Async XLA Ops:
  0.6 11.2 %copy-start = (f32[3,8,8,8,128]{4,3,2,1,0:T(8,128)S(1)}, f32[3,8,8,8,128]{4,3,2,1,0:T(8,128)}, u32[]{:S(2)}) copy-start(f32[3,8,8,8,128]{4,3,2,1,0:T(8,128)} %v_ref.2) | copy-start | bytes 2359300
  3.0 20.5 %all-to-all-start = ((f32[32,25,1,128]{3,2,1,0:T(1,128)}), f32[32,25,1,128]{3,2,1,0:T(1,128)S(1)}, u32[]{:S(2)}, u32[]{:S(2)}) async-start(f32[32,25,1,128]{3,2,1,0:T(1,128)} %bitcast.10), calls=%async_computation | async-start | bytes 819200 | tf_op jit(solution)/shard_map/all_to_all | solution.py:406
  11.8 1.0 %copy-start.1 = (f32[8,8,8,128]{3,2,1,0:T(8,128)S(1)}, f32[8,8,8,128]{3,2,1,0:T(8,128)}, u32[]{:S(2)}) copy-start(f32[8,8,8,128]{3,2,1,0:T(8,128)} %c_ref.3) | copy-start | bytes 786436
  13.6 7.0 %collective-permute-start.1 = (f32[128,128]{1,0:T(8,128)S(1)}, f32[128,128]{1,0:T(8,128)S(1)}, u32[]{:S(2)}, u32[]{:S(2)}) collective-permute-start(f32[128,128]{1,0:T(8,128)S(1)} %get-tuple-element.25.own_ref), channel_id=1, source_target_pairs={{1,0},{2,1},{3,2},{4,3},{5,4},{6,5},{7,6},{0,7},{9,8},{10,9},{11,1... | collective-permute-start | bytes 196616 | tf_op jit(solution)/shard_map/ppermute | solution.py:457
  19.2 4.3 %collective-permute-start = (f32[128,128]{1,0:T(8,128)S(1)}, f32[128,128]{1,0:T(8,128)S(1)}, u32[]{:S(2)}, u32[]{:S(2)}) collective-permute-start(f32[128,128]{1,0:T(8,128)S(1)} %get-tuple-element.25.own_ref), channel_id=1, source_target_pairs={{0,1},{1,2},{2,3},{3,4},{4,5},{5,6},{6,7},{7,0},{8,9},{9,10},{10,1... | collective-permute-start | bytes 196616 | tf_op jit(solution)/shard_map/ppermute | solution.py:456
  23.5 11.6 %copy-start.2 = (f32[8,8,8,128]{3,2,1,0:T(8,128)S(1)}, f32[8,8,8,128]{3,2,1,0:T(8,128)}, u32[]{:S(2)}) copy-start(f32[8,8,8,128]{3,2,1,0:T(8,128)} %c_ref.3) | copy-start | bytes 786436
  25.7 9.5 %copy-start.3 = (s32[24,128]{1,0:T(8,128)S(1)}, s32[24,128]{1,0:T(8,128)}, u32[]{:S(2)}) copy-start(s32[24,128]{1,0:T(8,128)} %get-tuple-element.32.meta_ref) | copy-start | bytes 36868
  25.7 16.7 %all-to-all-start.1 = ((f32[32,3,1,128]{3,2,1,0:T(1,128)}), f32[32,3,1,128]{3,2,1,0:T(1,128)S(1)}, u32[]{:S(2)}, u32[]{:S(2)}) async-start(f32[32,3,1,128]{3,2,1,0:T(1,128)} %bitcast.6), calls=%async_computation.1 | async-start | bytes 98304 | tf_op jit(solution)/shard_map/all_to_all | solution.py:406
  43.4 3.7 %collective-permute-start.3 = (f32[32,128]{1,0:T(8,128)S(1)}, f32[32,128]{1,0:T(8,128)S(1)}, u32[]{:S(2)}, u32[]{:S(2)}) collective-permute-start(f32[32,128]{1,0:T(8,128)S(1)} %get-tuple-element.43.low_ref), channel_id=1, source_target_pairs={{1,0},{2,1},{3,2},{4,3},{5,4},{6,5},{7,6},{0,7},{9,8},{10,9},{11,1... | collective-permute-start | bytes 49160 | tf_op jit(solution)/shard_map/ppermute | solution.py:473
  43.4 3.8 %collective-permute-start.2 = (f32[32,128]{1,0:T(8,128)S(1)}, f32[32,128]{1,0:T(8,128)S(1)}, u32[]{:S(2)}, u32[]{:S(2)}) collective-permute-start(f32[32,128]{1,0:T(8,128)S(1)} %get-tuple-element.44.high_ref), channel_id=1, source_target_pairs={{0,1},{1,2},{2,3},{3,4},{4,5},{5,6},{6,7},{7,0},{8,9},{9,10},{10,1... | collective-permute-start | bytes 49160 | tf_op jit(solution)/shard_map/ppermute | solution.py:472

commit v3 on v2

--- a/solution.py
+++ b/solution.py
@@ -141,7 +141,7 @@
     lax.fori_loop(0, turns, seven_peers, 0)
 
 
-def finish_kernel(reply_ref, meta_ref, value_ref, copy_ref, low_ref, high_ref):
+def finish_kernel(reply_ref, meta_ref, value_ref, low_ref, high_ref):
     sub = iota((8, 128), 0)
     planes = [[reply_ref[pl.ds(g * 24 + c, 8, stride=3), :] for g in range(4)] for c in range(3)]
     values = [[], [], []]
@@ -155,7 +155,6 @@
             values[c].append(jnp.sum(total, axis=0, keepdims=True))
     values = jnp.concatenate([jnp.concatenate(v, axis=1) for v in values], axis=0)
     value_ref[...] = values
-    copy_ref[...] = values
     target = jnp.concatenate([meta_ref[16 + r : 17 + r, :] for r in range(8)], axis=1)
     elem = target >> 9
     zx = ((target >> 6) & 7) * 8 + (target & 7)
@@ -313,8 +312,55 @@
     one_pass(*coefs, buf_ref, out_ref)
 
 
-def main_kernel(value_ref, meta_ref, node_ref, base_ref, w_ref, c_ref, out_ref, add_ref, one_ref, two_ref, dl_ref):
+def prepare_edge(own_ref, below_ref, above_ref, edge_ref):
+    even, joined = edge_masks()
+    sub = iota((8, 128), 0)
+    y_of = (iota((8, 128), 1) >> 1) & 7
+    v = edge_stack(own_ref, below_ref, above_ref, 0, even)
+    k = [H_STIFF * c for c in edge_stack(own_ref, below_ref, above_ref, 64, even)]
+    ky = [jnp.where(y_of < 7, k[i], 0.0) for i in range(16)]
+    kx = [jnp.where(sub < 7, k[i], 0.0) for i in range(16)]
+    diag = []
+    for i in range(16):
+        d = H_MASS + kx[i] + pltpu.roll(kx[i], 1, 0) + ky[i] + pltpu.roll(ky[i], 2, 1)
+        if i % 8 < 7:
+            d = d + k[i]
+        if i % 8 > 0:
+            d = d + k[i - 1]
+        diag.append(d)
+    d7, d8 = diag[7], diag[8]
+    edge_ref[5, 0] = d7
+    edge_ref[5, 1] = d8
+    diag[7], diag[8] = d7 + jnp.where(joined, d8, 0.0), d8 + jnp.where(joined, d7, 0.0)
+    for i in range(16):
+        edge_ref[0, i] = v[i]
+        edge_ref[1, i] = k[i]
+        edge_ref[2, i] = ky[i]
+        edge_ref[3, i] = kx[i]
+        edge_ref[4, i] = OMEGA / diag[i]
+
+
+def main_kernel(
+    value_ref,
+    meta_ref,
+    node_ref,
+    base_ref,
+    w_ref,
+    c_ref,
+    own_ref,
+    below_ref,
+    above_ref,
+    value_out_ref,
+    out_ref,
+    edge_ref,
+    add_ref,
+    one_ref,
+    two_ref,
+    dl_ref,
+):
     lane = iota((8, 128), 1)
+    value_out_ref[...] = value_ref[...]
+    prepare_edge(own_ref, below_ref, above_ref, edge_ref)
     target = jnp.concatenate([meta_ref[16 + r : 17 + r, :] for r in range(8)], axis=1)
     elem_hot = jnp.where((target >> 9) == iota((128, 1024), 0), 1.0, 0.0).astype(BF16)
     for c in range(3):
@@ -346,14 +392,12 @@
 
 
 def edge_kernel(
-    main_ref, own_ref, below_ref, above_ref, low_ref, high_ref, add_below_ref, add_above_ref, out_hbm, out_ref, sems
+    main_ref, edge_ref, low_ref, high_ref, add_below_ref, add_above_ref, out_hbm, out_ref, sems
 ):
     lane = iota((8, 128), 1)
-    sub = iota((8, 128), 0)
     even, joined = edge_masks()
-    y_of = (lane >> 1) & 7
-    v = edge_stack(own_ref, below_ref, above_ref, 0, even)
-    k = [H_STIFF * c for c in edge_stack(own_ref, below_ref, above_ref, 64, even)]
+    v, k, ky, kx, w = [[edge_ref[n, i] for i in range(16)] for n in range(5)]
+    d7, d8 = edge_ref[5, 0], edge_ref[5, 1]
     rhs = [H_MASS * v[i] for i in range(16)]
     for z in range(8):
         part, rows = (low_ref, high_ref)[z // 4], slice(z % 4 * 8, z % 4 * 8 + 8)
@@ -365,19 +409,6 @@
             upper = jnp.where(even, pltpu.roll(add_above_ref[rows, :], 127, 1), mine)
         rhs[z] = rhs[z] + lower
         rhs[8 + z] = rhs[8 + z] + upper
-    ky = [jnp.where(y_of < 7, k[i], 0.0) for i in range(16)]
-    kx = [jnp.where(sub < 7, k[i], 0.0) for i in range(16)]
-    diag = []
-    for i in range(16):
-        d = H_MASS + kx[i] + pltpu.roll(kx[i], 1, 0) + ky[i] + pltpu.roll(ky[i], 2, 1)
-        if i % 8 < 7:
-            d = d + k[i]
-        if i % 8 > 0:
-            d = d + k[i - 1]
-        diag.append(d)
-    d7, d8 = diag[7], diag[8]
-    diag[7], diag[8] = d7 + jnp.where(joined, d8, 0.0), d8 + jnp.where(joined, d7, 0.0)
-    w = [OMEGA / d for d in diag]
     now = v
     for number in range(NPASS):
         now = edge_pass(number, now, rhs, k, ky, kx, w, d7, d8, joined)
@@ -466,21 +497,21 @@
         [pltpu.VMEM((3,) + plane, F32), pltpu.VMEM((2, 8, 8, 128), F32)],
     )
     reply, base, w, nodes = lax.optimization_barrier((reply, base, w, nodes))
-    iface_values, values, add_low, add_high = call(
-        finish_kernel, [sds(3, 1024), sds(3, 1024), sds(32, 128), sds(32, 128)], [reply, meta]
+    values, add_low, add_high = call(
+        finish_kernel, [sds(3, 1024), sds(32, 128), sds(32, 128)], [reply, meta]
     )
     add_below = lax.ppermute(add_high, "blk", up)
     add_above = lax.ppermute(add_low, "blk", down)
-    main = call(
+    iface_values, main, edge = call(
         main_kernel,
-        [sds(3, *plane)],
-        [values, meta, nodes, base, w, c_later],
+        [sds(3, 1024), sds(3, *plane), sds(6, 16, 8, 128)],
+        [values, meta, nodes, base, w, c_later, own, below, above],
         [pltpu.VMEM((3,) + plane, F32)] * 3 + [pltpu.VMEM((2, 8, 8, 128), F32)],
     )
     field = call(
         edge_kernel,
         [sds(3, *plane)],
-        [main, own, below, above, add_low, add_high, add_below, add_above],
+        [main, edge, add_low, add_high, add_below, add_above],
         [pltpu.VMEM((3,) + plane, F32), pltpu.SemaphoreType.DMA((6,))],
         out_space=pl.ANY,
     )

time: 49.1 us -> 49.2 us (level)
  transfers between devices with their start and end apart: 6 -> 6, of which waited for: 4 -> 3; matrix products, arithmetic and copies ran while one was open for 0% -> 0% of each run, Pallas kernels for 11% -> 13%
where the time goes in v3:
time: 49.2 us; the launch traced here: 48.9 us
  starting transfers between devices  25.5 us (52%)
  Pallas kernels  12.7 us (26%)
  waiting for transfers between devices  9.06 us (18%)
  local copies, waits for them, and re-layouts  0.96 us (2%)
  between operations  0.73 us (1%)
    all_to_all x2, starting transfers between devices, exchange(): lax.all_to_all(chunks, 'sess', 0, 0, tiled=True).reshape(PEERS * count, 128)  18.3 us
    pallas_call x7, Pallas kernels, call(): pl.pallas_call(kernel, out_shape=outs[0] if single else outs, in_specs=[p...  12.7 us
    ppermute x1, starting transfers between devices, body(): above = lax.ppermute(own, 'blk', down)  5.65 us
    all_to_all x2, waiting for transfers between devices, exchange(): lax.all_to_all(chunks, 'sess', 0, 0, tiled=True).reshape(PEERS * count, 128)  4.73 us
    ppermute x1, waiting for transfers between devices, body(): below = lax.ppermute(own, 'blk', up)  2.99 us
    ppermute x1, starting transfers between devices, body(): add_below = lax.ppermute(add_high, 'blk', up)  1.45 us
    ppermute x1, waiting for transfers between devices, body(): above = lax.ppermute(own, 'blk', down)  1.33 us
  transfers between devices with their start and end apart: 6, of which 3 were waited for; matrix products, arithmetic and copies ran while one was open for 0% of the time, Pallas kernels for 13%

profile of v3, /device:TPU:1, one launch (start us, length us, event | category | flops | bytes accessed | tf_op | source)
XLA Modules:
  0.0 48.9 jit_solution(6234970125086171324)
XLA Ops:
  0.6 0.0 copy-start
  0.6 2.4 %shard_map.77 = (f32[800,128]{1,0:T(8,128)}, s32[24,128]{1,0:T(8,128)}) custom-call(s32[8,128]{1,0:T(8,128)} %bitcast.12, s32[8,128]{1,0:T(8,128)} %bitcast.13, f32[24,1024]{1,0:T(8,128)} %bitcast.11, s32[8,128]{1,0:T(8,128)} %bitcast.14), custom_call_target="tpu_custom_call" | custom-call | tf_op jit(solution)/shard_map/pallas_call | solution.py:443
  3.0 8.8 %all-to-all-start = ((f32[32,25,1,128]{3,2,1,0:T(1,128)}), f32[32,25,1,128]{3,2,1,0:T(1,128)S(1)}, u32[]{:S(2)}, u32[]{:S(2)}) async-start(f32[32,25,1,128]{3,2,1,0:T(1,128)} %bitcast.10), calls=%async_computation | async-start | bytes 819200 | tf_op jit(solution)/shard_map/all_to_all | solution.py:437
  11.8 0.0 copy-done
  11.8 0.0 copy-start.1
  11.9 0.9 %copy-done.1 = f32[8,8,8,128]{3,2,1,0:T(8,128)S(1)} copy-done((f32[8,8,8,128]{3,2,1,0:T(8,128)S(1)}, f32[8,8,8,128]{3,2,1,0:T(8,128)}, u32[]{:S(2)}) %copy-start.1) | copy-done | bytes 262168
  12.8 0.8 %shard_map.78 = (f32[128,128]{1,0:T(8,128)S(1)}, bf16[1024,256]{1,0:T(8,128)(2,1)S(1)}, f32[8,8,8,128]{3,2,1,0:T(8,128)S(1)}) custom-call(f32[3,8,8,8,128]{4,3,2,1,0:T(8,128)S(1)} %copy-done, f32[8,8,8,128]{3,2,1,0:T(8,128)S(1)} %copy-done.1), custom_call_target="tpu_custom_call" | custom-call | tf_op jit(solution)/shard_map/pallas_call | solution.py:443
  13.6 5.7 %collective-permute-start.1 = (f32[128,128]{1,0:T(8,128)S(1)}, f32[128,128]{1,0:T(8,128)S(1)}, u32[]{:S(2)}, u32[]{:S(2)}) collective-permute-start(f32[128,128]{1,0:T(8,128)S(1)} %get-tuple-element.27.own_ref), channel_id=1, source_target_pairs={{1,0},{2,1},{3,2},{4,3},{5,4},{6,5},{7,6},{0,7},{9,8},{10,9},{11,1... | collective-permute-start | bytes 196616 | tf_op jit(solution)/shard_map/ppermute | solution.py:488
  19.2 0.0 collective-permute-start
  19.2 1.3 %collective-permute-done.1.above_ref = f32[128,128]{1,0:T(8,128)S(1)} collective-permute-done((f32[128,128]{1,0:T(8,128)S(1)}, f32[128,128]{1,0:T(8,128)S(1)}, u32[]{:S(2)}, u32[]{:S(2)}) %collective-permute-start.1) | collective-permute-done | bytes 65568 | tf_op jit(solution)/shard_map/ppermute | solution.py:488
  20.6 3.0 %collective-permute-done.below_ref = f32[128,128]{1,0:T(8,128)S(1)} collective-permute-done((f32[128,128]{1,0:T(8,128)S(1)}, f32[128,128]{1,0:T(8,128)S(1)}, u32[]{:S(2)}, u32[]{:S(2)}) %collective-permute-start) | collective-permute-done | bytes 65568 | tf_op jit(solution)/shard_map/ppermute | solution.py:487
  23.5 0.0 all-to-all-done
  23.6 2.2 %shard_map.79 = f32[96,128]{1,0:T(8,128)} custom-call(f32[800,128]{1,0:T(8,128)S(1)} %bitcast.8, bf16[1024,256]{1,0:T(8,128)(2,1)S(1)} %get-tuple-element.29.split_ref, f32[8,8,8,128]{3,2,1,0:T(8,128)S(1)} %get-tuple-element.30.first_ref), custom_call_target="tpu_custom_call" | custom-call | tf_op jit(solution)/shard_map/pallas_call | solution.py:443
  25.7 9.4 %all-to-all-start.1 = ((f32[32,3,1,128]{3,2,1,0:T(1,128)}), f32[32,3,1,128]{3,2,1,0:T(1,128)S(1)}, u32[]{:S(2)}, u32[]{:S(2)}) async-start(f32[32,3,1,128]{3,2,1,0:T(1,128)} %bitcast.6), calls=%async_computation.1 | async-start | bytes 98304 | tf_op jit(solution)/shard_map/all_to_all | solution.py:437
  35.2 0.0 copy-done.2
  35.2 2.5 %shard_map.80 = (f32[3,8,8,8,128]{4,3,2,1,0:T(8,128)S(1)}, f32[8,8,8,128]{3,2,1,0:T(8,128)S(1)}, bf16[512,1024]{1,0:T(8,128)(2,1)S(1)}) custom-call(f32[3,8,8,8,128]{4,3,2,1,0:T(8,128)S(1)} %copy-done, f32[8,8,8,128]{3,2,1,0:T(8,128)S(1)} %copy-done.2, s32[24,128]{1,0:T(8,128)S(1)} %copy-done.3), custom_call_target="tpu_custom_call" | custom-call | tf_op jit(solution)/shard_map/pallas_call | solution.py:443
  37.7 4.7 %all-to-all-done.1 = f32[32,3,1,128]{3,2,1,0:T(1,128)S(1)} async-done(((f32[32,3,1,128]{3,2,1,0:T(1,128)}), f32[32,3,1,128]{3,2,1,0:T(1,128)S(1)}, u32[]{:S(2)}, u32[]{:S(2)}) %all-to-all-start.1) | async-done | bytes 49184 | tf_op jit(solution)/shard_map/all_to_all | solution.py:437
  42.5 0.5 %shard_map.81 = (f32[3,1024]{1,0:T(4,128)S(1)}, f32[32,128]{1,0:T(8,128)S(1)}, f32[32,128]{1,0:T(8,128)S(1)}) custom-call(f32[96,128]{1,0:T(8,128)S(1)} %bitcast.9, s32[24,128]{1,0:T(8,128)S(1)} %copy-done.3), custom_call_target="tpu_custom_call" | custom-call | tf_op jit(solution)/shard_map/pallas_call | solution.py:443
  43.0 0.1 collective-permute-start.3
  43.1 1.5 %collective-permute-start.2 = (f32[32,128]{1,0:T(8,128)S(1)}, f32[32,128]{1,0:T(8,128)S(1)}, u32[]{:S(2)}, u32[]{:S(2)}) collective-permute-start(f32[32,128]{1,0:T(8,128)S(1)} %get-tuple-element.48.high_ref), channel_id=1, source_target_pairs={{0,1},{1,2},{2,3},{3,4},{4,5},{5,6},{6,7},{7,0},{8,9},{9,10},{10,1... | collective-permute-start | bytes 49160 | tf_op jit(solution)/shard_map/ppermute | solution.py:503
  44.6 2.8 %shard_map.82 = (f32[3,1024]{1,0:T(4,128)}, f32[3,8,8,8,128]{4,3,2,1,0:T(8,128)S(1)}, f32[6,16,8,128]{3,2,1,0:T(8,128)S(1)}) custom-call(f32[3,1024]{1,0:T(4,128)S(1)} %get-tuple-element.39.value_ref, s32[24,128]{1,0:T(8,128)S(1)} %copy-done.3, bf16[512,1024]{1,0:T(8,128)(2,1)S(1)} %get-tuple-element.40.node_ref, ...), custom_call_target="tpu_custom_call" | custom-call | tf_op jit(solution)/shard_map/pallas_call | solution.py:443
  47.4 0.0 collective-permute-done.3.add_above_ref
  47.4 0.0 collective-permute-done.2.add_below_ref
  47.4 1.5 %shard_map.83 = f32[3,8,8,8,128]{4,3,2,1,0:T(8,128)} custom-call(f32[3,8,8,8,128]{4,3,2,1,0:T(8,128)S(1)} %get-tuple-element.45.main_ref, f32[6,16,8,128]{3,2,1,0:T(8,128)S(1)} %get-tuple-element.46.edge_ref, f32[32,128]{1,0:T(8,128)S(1)} %get-tuple-element.47.low_ref, f32[32,128]{1,0:T(8,128)S(1)} %get-tuple-element.48.high_ref, ...), custom_call_target="tpu_custom_call" | custom-call | tf_op jit(solution)/shard_map/pallas_call | solution.py:443
  (3 shorter events, 0.0 us)
Async XLA Ops:
  0.6 11.2 %copy-start = (f32[3,8,8,8,128]{4,3,2,1,0:T(8,128)S(1)}, f32[3,8,8,8,128]{4,3,2,1,0:T(8,128)}, u32[]{:S(2)}) copy-start(f32[3,8,8,8,128]{4,3,2,1,0:T(8,128)} %v_ref.2) | copy-start | bytes 2359300
  3.0 20.5 %all-to-all-start = ((f32[32,25,1,128]{3,2,1,0:T(1,128)}), f32[32,25,1,128]{3,2,1,0:T(1,128)S(1)}, u32[]{:S(2)}, u32[]{:S(2)}) async-start(f32[32,25,1,128]{3,2,1,0:T(1,128)} %bitcast.10), calls=%async_computation | async-start | bytes 819200 | tf_op jit(solution)/shard_map/all_to_all | solution.py:437
  11.8 1.0 %copy-start.1 = (f32[8,8,8,128]{3,2,1,0:T(8,128)S(1)}, f32[8,8,8,128]{3,2,1,0:T(8,128)}, u32[]{:S(2)}) copy-start(f32[8,8,8,128]{3,2,1,0:T(8,128)} %c_ref.3) | copy-start | bytes 786436
  13.6 7.0 %collective-permute-start.1 = (f32[128,128]{1,0:T(8,128)S(1)}, f32[128,128]{1,0:T(8,128)S(1)}, u32[]{:S(2)}, u32[]{:S(2)}) collective-permute-start(f32[128,128]{1,0:T(8,128)S(1)} %get-tuple-element.27.own_ref), channel_id=1, source_target_pairs={{1,0},{2,1},{3,2},{4,3},{5,4},{6,5},{7,6},{0,7},{9,8},{10,9},{11,1... | collective-permute-start | bytes 196616 | tf_op jit(solution)/shard_map/ppermute | solution.py:488
  19.2 4.3 %collective-permute-start = (f32[128,128]{1,0:T(8,128)S(1)}, f32[128,128]{1,0:T(8,128)S(1)}, u32[]{:S(2)}, u32[]{:S(2)}) collective-permute-start(f32[128,128]{1,0:T(8,128)S(1)} %get-tuple-element.27.own_ref), channel_id=1, source_target_pairs={{0,1},{1,2},{2,3},{3,4},{4,5},{5,6},{6,7},{7,0},{8,9},{9,10},{10,1... | collective-permute-start | bytes 196616 | tf_op jit(solution)/shard_map/ppermute | solution.py:487
  23.5 11.6 %copy-start.2 = (f32[8,8,8,128]{3,2,1,0:T(8,128)S(1)}, f32[8,8,8,128]{3,2,1,0:T(8,128)}, u32[]{:S(2)}) copy-start(f32[8,8,8,128]{3,2,1,0:T(8,128)} %c_ref.3) | copy-start | bytes 786436
  25.7 9.5 %copy-start.3 = (s32[24,128]{1,0:T(8,128)S(1)}, s32[24,128]{1,0:T(8,128)}, u32[]{:S(2)}) copy-start(s32[24,128]{1,0:T(8,128)} %get-tuple-element.34.meta_ref) | copy-start | bytes 36868
  25.7 16.7 %all-to-all-start.1 = ((f32[32,3,1,128]{3,2,1,0:T(1,128)}), f32[32,3,1,128]{3,2,1,0:T(1,128)S(1)}, u32[]{:S(2)}, u32[]{:S(2)}) async-start(f32[32,3,1,128]{3,2,1,0:T(1,128)} %bitcast.6), calls=%async_computation.1 | async-start | bytes 98304 | tf_op jit(solution)/shard_map/all_to_all | solution.py:437
  43.0 4.4 %collective-permute-start.3 = (f32[32,128]{1,0:T(8,128)S(1)}, f32[32,128]{1,0:T(8,128)S(1)}, u32[]{:S(2)}, u32[]{:S(2)}) collective-permute-start(f32[32,128]{1,0:T(8,128)S(1)} %get-tuple-element.47.low_ref), channel_id=1, source_target_pairs={{1,0},{2,1},{3,2},{4,3},{5,4},{6,5},{7,6},{0,7},{9,8},{10,9},{11,1... | collective-permute-start | bytes 49160 | tf_op jit(solution)/shard_map/ppermute | solution.py:504
  43.1 4.3 %collective-permute-start.2 = (f32[32,128]{1,0:T(8,128)S(1)}, f32[32,128]{1,0:T(8,128)S(1)}, u32[]{:S(2)}, u32[]{:S(2)}) collective-permute-start(f32[32,128]{1,0:T(8,128)S(1)} %get-tuple-element.48.high_ref), channel_id=1, source_target_pairs={{0,1},{1,2},{2,3},{3,4},{4,5},{5,6},{6,7},{7,0},{8,9},{9,10},{10,1... | collective-permute-start | bytes 49160 | tf_op jit(solution)/shard_map/ppermute | solution.py:503

commit v4 on v2

--- a/solution.py
+++ b/solution.py
@@ -141,7 +141,7 @@
     lax.fori_loop(0, turns, seven_peers, 0)
 
 
-def finish_kernel(reply_ref, meta_ref, value_ref, copy_ref, low_ref, high_ref):
+def finish_kernel(reply_ref, meta_ref, value_ref, low_ref, high_ref):
     sub = iota((8, 128), 0)
     planes = [[reply_ref[pl.ds(g * 24 + c, 8, stride=3), :] for g in range(4)] for c in range(3)]
     values = [[], [], []]
@@ -155,7 +155,6 @@
             values[c].append(jnp.sum(total, axis=0, keepdims=True))
     values = jnp.concatenate([jnp.concatenate(v, axis=1) for v in values], axis=0)
     value_ref[...] = values
-    copy_ref[...] = values
     target = jnp.concatenate([meta_ref[16 + r : 17 + r, :] for r in range(8)], axis=1)
     elem = target >> 9
     zx = ((target >> 6) & 7) * 8 + (target & 7)
@@ -346,8 +345,22 @@
 
 
 def edge_kernel(
-    main_ref, own_ref, below_ref, above_ref, low_ref, high_ref, add_below_ref, add_above_ref, out_hbm, out_ref, sems
+    main_ref,
+    own_ref,
+    below_ref,
+    above_ref,
+    low_ref,
+    high_ref,
+    add_below_ref,
+    add_above_ref,
+    value_ref,
+    out_hbm,
+    value_hbm,
+    out_ref,
+    sems,
 ):
+    copies = [pltpu.make_async_copy(value_ref, value_hbm, sems.at[6])]
+    copies[0].start()
     lane = iota((8, 128), 1)
     sub = iota((8, 128), 0)
     even, joined = edge_masks()
@@ -381,7 +394,6 @@
     now = v
     for number in range(NPASS):
         now = edge_pass(number, now, rhs, k, ky, kx, w, d7, d8, joined)
-    copies = []
     for c in range(3):
         for half in range(2):
             planes = slice(half * 4, half * 4 + 4)
@@ -466,8 +478,8 @@
         [pltpu.VMEM((3,) + plane, F32), pltpu.VMEM((2, 8, 8, 128), F32)],
     )
     reply, base, w, nodes = lax.optimization_barrier((reply, base, w, nodes))
-    iface_values, values, add_low, add_high = call(
-        finish_kernel, [sds(3, 1024), sds(3, 1024), sds(32, 128), sds(32, 128)], [reply, meta]
+    values, add_low, add_high = call(
+        finish_kernel, [sds(3, 1024), sds(32, 128), sds(32, 128)], [reply, meta]
     )
     add_below = lax.ppermute(add_high, "blk", up)
     add_above = lax.ppermute(add_low, "blk", down)
@@ -477,11 +489,11 @@
         [values, meta, nodes, base, w, c_later],
         [pltpu.VMEM((3,) + plane, F32)] * 3 + [pltpu.VMEM((2, 8, 8, 128), F32)],
     )
-    field = call(
+    field, iface_values = call(
         edge_kernel,
-        [sds(3, *plane)],
-        [main, own, below, above, add_low, add_high, add_below, add_above],
-        [pltpu.VMEM((3,) + plane, F32), pltpu.SemaphoreType.DMA((6,))],
+        [sds(3, *plane), sds(3, 1024)],
+        [main, own, below, above, add_low, add_high, add_below, add_above, values],
+        [pltpu.VMEM((3,) + plane, F32), pltpu.SemaphoreType.DMA((7,))],
         out_space=pl.ANY,
     )
     return field, iface_values

time: 49.1 us -> 48.9 us (level)
  no operation moved by 1% of the time
where the time goes in v4:
time: 48.9 us; the launch traced here: 48.6 us
  starting transfers between devices  25.5 us (52%)
  Pallas kernels  12.2 us (25%)
  waiting for transfers between devices  9.19 us (19%)
  local copies, waits for them, and re-layouts  0.96 us (2%)
  between operations  0.74 us (2%)
    all_to_all x2, starting transfers between devices, exchange(): lax.all_to_all(chunks, 'sess', 0, 0, tiled=True).reshape(PEERS * count, 128)  18.3 us
    pallas_call x7, Pallas kernels, call(): pl.pallas_call(kernel, out_shape=outs[0] if single else outs, in_specs=[p...  12.2 us
    ppermute x1, starting transfers between devices, body(): above = lax.ppermute(own, 'blk', down)  5.65 us
    all_to_all x2, waiting for transfers between devices, exchange(): lax.all_to_all(chunks, 'sess', 0, 0, tiled=True).reshape(PEERS * count, 128)  4.73 us
    ppermute x1, waiting for transfers between devices, body(): below = lax.ppermute(own, 'blk', up)  2.99 us
    ppermute x1, starting transfers between devices, body(): add_below = lax.ppermute(add_high, 'blk', up)  1.45 us
    ppermute x1, waiting for transfers between devices, body(): above = lax.ppermute(own, 'blk', down)  1.33 us
  transfers between devices with their start and end apart: 6, of which 4 were waited for; matrix products, arithmetic and copies ran while one was open for 0% of the time, Pallas kernels for 11%

profile of v4, /device:TPU:1, one launch (start us, length us, event | category | flops | bytes accessed | tf_op | source)
XLA Modules:
  0.0 48.6 jit_solution(7390377170234582742)
XLA Ops:
  0.6 0.0 copy-start
  0.6 2.4 %shard_map.77 = (f32[800,128]{1,0:T(8,128)}, s32[24,128]{1,0:T(8,128)}) custom-call(s32[8,128]{1,0:T(8,128)} %bitcast.12, s32[8,128]{1,0:T(8,128)} %bitcast.13, f32[24,1024]{1,0:T(8,128)} %bitcast.11, s32[8,128]{1,0:T(8,128)} %bitcast.14), custom_call_target="tpu_custom_call" | custom-call | tf_op jit(solution)/shard_map/pallas_call | solution.py:424
  3.0 8.8 %all-to-all-start = ((f32[32,25,1,128]{3,2,1,0:T(1,128)}), f32[32,25,1,128]{3,2,1,0:T(1,128)S(1)}, u32[]{:S(2)}, u32[]{:S(2)}) async-start(f32[32,25,1,128]{3,2,1,0:T(1,128)} %bitcast.10), calls=%async_computation | async-start | bytes 819200 | tf_op jit(solution)/shard_map/all_to_all | solution.py:418
  11.8 0.0 copy-done
  11.8 0.0 copy-start.1
  11.9 0.9 %copy-done.1 = f32[8,8,8,128]{3,2,1,0:T(8,128)S(1)} copy-done((f32[8,8,8,128]{3,2,1,0:T(8,128)S(1)}, f32[8,8,8,128]{3,2,1,0:T(8,128)}, u32[]{:S(2)}) %copy-start.1) | copy-done | bytes 262168
  12.8 0.8 %shard_map.78 = (f32[128,128]{1,0:T(8,128)S(1)}, bf16[1024,256]{1,0:T(8,128)(2,1)S(1)}, f32[8,8,8,128]{3,2,1,0:T(8,128)S(1)}) custom-call(f32[3,8,8,8,128]{4,3,2,1,0:T(8,128)S(1)} %copy-done, f32[8,8,8,128]{3,2,1,0:T(8,128)S(1)} %copy-done.1), custom_call_target="tpu_custom_call" | custom-call | tf_op jit(solution)/shard_map/pallas_call | solution.py:424
  13.6 5.7 %collective-permute-start.1 = (f32[128,128]{1,0:T(8,128)S(1)}, f32[128,128]{1,0:T(8,128)S(1)}, u32[]{:S(2)}, u32[]{:S(2)}) collective-permute-start(f32[128,128]{1,0:T(8,128)S(1)} %get-tuple-element.24.own_ref), channel_id=1, source_target_pairs={{1,0},{2,1},{3,2},{4,3},{5,4},{6,5},{7,6},{0,7},{9,8},{10,9},{11,1... | collective-permute-start | bytes 196616 | tf_op jit(solution)/shard_map/ppermute | solution.py:469
  19.2 0.0 collective-permute-start
  19.2 1.3 %collective-permute-done.1.above_ref = f32[128,128]{1,0:T(8,128)S(1)} collective-permute-done((f32[128,128]{1,0:T(8,128)S(1)}, f32[128,128]{1,0:T(8,128)S(1)}, u32[]{:S(2)}, u32[]{:S(2)}) %collective-permute-start.1) | collective-permute-done | bytes 65568 | tf_op jit(solution)/shard_map/ppermute | solution.py:469
  20.6 3.0 %collective-permute-done.below_ref = f32[128,128]{1,0:T(8,128)S(1)} collective-permute-done((f32[128,128]{1,0:T(8,128)S(1)}, f32[128,128]{1,0:T(8,128)S(1)}, u32[]{:S(2)}, u32[]{:S(2)}) %collective-permute-start) | collective-permute-done | bytes 65568 | tf_op jit(solution)/shard_map/ppermute | solution.py:468
  23.5 0.0 all-to-all-done
  23.6 2.2 %shard_map.79 = f32[96,128]{1,0:T(8,128)} custom-call(f32[800,128]{1,0:T(8,128)S(1)} %bitcast.8, bf16[1024,256]{1,0:T(8,128)(2,1)S(1)} %get-tuple-element.26.split_ref, f32[8,8,8,128]{3,2,1,0:T(8,128)S(1)} %get-tuple-element.27.first_ref), custom_call_target="tpu_custom_call" | custom-call | tf_op jit(solution)/shard_map/pallas_call | solution.py:424
  25.7 9.4 %all-to-all-start.1 = ((f32[32,3,1,128]{3,2,1,0:T(1,128)}), f32[32,3,1,128]{3,2,1,0:T(1,128)S(1)}, u32[]{:S(2)}, u32[]{:S(2)}) async-start(f32[32,3,1,128]{3,2,1,0:T(1,128)} %bitcast.6), calls=%async_computation.1 | async-start | bytes 98304 | tf_op jit(solution)/shard_map/all_to_all | solution.py:418
  35.2 0.0 copy-done.2
  35.2 2.5 %shard_map.80 = (f32[3,8,8,8,128]{4,3,2,1,0:T(8,128)S(1)}, f32[8,8,8,128]{3,2,1,0:T(8,128)S(1)}, bf16[512,1024]{1,0:T(8,128)(2,1)S(1)}) custom-call(f32[3,8,8,8,128]{4,3,2,1,0:T(8,128)S(1)} %copy-done, f32[8,8,8,128]{3,2,1,0:T(8,128)S(1)} %copy-done.2, s32[24,128]{1,0:T(8,128)S(1)} %copy-done.3), custom_call_target="tpu_custom_call" | custom-call | tf_op jit(solution)/shard_map/pallas_call | solution.py:424
  37.7 4.7 %all-to-all-done.1 = f32[32,3,1,128]{3,2,1,0:T(1,128)S(1)} async-done(((f32[32,3,1,128]{3,2,1,0:T(1,128)}), f32[32,3,1,128]{3,2,1,0:T(1,128)S(1)}, u32[]{:S(2)}, u32[]{:S(2)}) %all-to-all-start.1) | async-done | bytes 49184 | tf_op jit(solution)/shard_map/all_to_all | solution.py:418
  42.5 0.5 %shard_map.81 = (f32[3,1024]{1,0:T(4,128)S(1)}, f32[32,128]{1,0:T(8,128)S(1)}, f32[32,128]{1,0:T(8,128)S(1)}) custom-call(f32[96,128]{1,0:T(8,128)S(1)} %bitcast.9, s32[24,128]{1,0:T(8,128)S(1)} %copy-done.3), custom_call_target="tpu_custom_call" | custom-call | tf_op jit(solution)/shard_map/pallas_call | solution.py:424
  43.0 0.1 collective-permute-start.3
  43.1 1.5 %collective-permute-start.2 = (f32[32,128]{1,0:T(8,128)S(1)}, f32[32,128]{1,0:T(8,128)S(1)}, u32[]{:S(2)}, u32[]{:S(2)}) collective-permute-start(f32[32,128]{1,0:T(8,128)S(1)} %get-tuple-element.43.high_ref), channel_id=1, source_target_pairs={{0,1},{1,2},{2,3},{3,4},{4,5},{5,6},{6,7},{7,0},{8,9},{9,10},{10,1... | collective-permute-start | bytes 49160 | tf_op jit(solution)/shard_map/ppermute | solution.py:484
  44.6 2.3 %shard_map.82.main_ref = f32[3,8,8,8,128]{4,3,2,1,0:T(8,128)S(1)} custom-call(f32[3,1024]{1,0:T(4,128)S(1)} %get-tuple-element.36.value_ref, s32[24,128]{1,0:T(8,128)S(1)} %copy-done.3, bf16[512,1024]{1,0:T(8,128)(2,1)S(1)} %get-tuple-element.37.node_ref, f32[3,8,8,8,128]{4,3,2,1,0:T(8,128)S(1)} %get-tuple-element.38.base_ref, ...), custom_call_target="tpu_custom_call" | custom-call | tf_op jit(solution)/shard_map/pallas_call | solution.py:424
  46.8 0.0 collective-permute-done.3.add_above_ref
  46.8 0.1 collective-permute-done.2.add_below_ref
  47.0 1.6 %shard_map.83 = (f32[3,8,8,8,128]{4,3,2,1,0:T(8,128)}, f32[3,1024]{1,0:T(4,128)}) custom-call(f32[3,8,8,8,128]{4,3,2,1,0:T(8,128)S(1)} %shard_map.82.main_ref, f32[128,128]{1,0:T(8,128)S(1)} %get-tuple-element.24.own_ref, f32[128,128]{1,0:T(8,128)S(1)} %collective-permute-done.below_ref, f32[128,128]{1,0:T(8,128)S(1)} %collective-permute-done.1.above_ref, ...), custom_call_target="tpu_custom_call" | custom-call | tf_op jit(solution)/shard_map/pallas_call | solution.py:424
  (3 shorter events, 0.0 us)
Async XLA Ops:
  0.6 11.2 %copy-start = (f32[3,8,8,8,128]{4,3,2,1,0:T(8,128)S(1)}, f32[3,8,8,8,128]{4,3,2,1,0:T(8,128)}, u32[]{:S(2)}) copy-start(f32[3,8,8,8,128]{4,3,2,1,0:T(8,128)} %v_ref.2) | copy-start | bytes 2359300
  3.0 20.5 %all-to-all-start = ((f32[32,25,1,128]{3,2,1,0:T(1,128)}), f32[32,25,1,128]{3,2,1,0:T(1,128)S(1)}, u32[]{:S(2)}, u32[]{:S(2)}) async-start(f32[32,25,1,128]{3,2,1,0:T(1,128)} %bitcast.10), calls=%async_computation | async-start | bytes 819200 | tf_op jit(solution)/shard_map/all_to_all | solution.py:418
  11.8 1.0 %copy-start.1 = (f32[8,8,8,128]{3,2,1,0:T(8,128)S(1)}, f32[8,8,8,128]{3,2,1,0:T(8,128)}, u32[]{:S(2)}) copy-start(f32[8,8,8,128]{3,2,1,0:T(8,128)} %c_ref.3) | copy-start | bytes 786436
  13.6 7.0 %collective-permute-start.1 = (f32[128,128]{1,0:T(8,128)S(1)}, f32[128,128]{1,0:T(8,128)S(1)}, u32[]{:S(2)}, u32[]{:S(2)}) collective-permute-start(f32[128,128]{1,0:T(8,128)S(1)} %get-tuple-element.24.own_ref), channel_id=1, source_target_pairs={{1,0},{2,1},{3,2},{4,3},{5,4},{6,5},{7,6},{0,7},{9,8},{10,9},{11,1... | collective-permute-start | bytes 196616 | tf_op jit(solution)/shard_map/ppermute | solution.py:469
  19.2 4.3 %collective-permute-start = (f32[128,128]{1,0:T(8,128)S(1)}, f32[128,128]{1,0:T(8,128)S(1)}, u32[]{:S(2)}, u32[]{:S(2)}) collective-permute-start(f32[128,128]{1,0:T(8,128)S(1)} %get-tuple-element.24.own_ref), channel_id=1, source_target_pairs={{0,1},{1,2},{2,3},{3,4},{4,5},{5,6},{6,7},{7,0},{8,9},{9,10},{10,1... | collective-permute-start | bytes 196616 | tf_op jit(solution)/shard_map/ppermute | solution.py:468
  23.5 11.6 %copy-start.2 = (f32[8,8,8,128]{3,2,1,0:T(8,128)S(1)}, f32[8,8,8,128]{3,2,1,0:T(8,128)}, u32[]{:S(2)}) copy-start(f32[8,8,8,128]{3,2,1,0:T(8,128)} %c_ref.3) | copy-start | bytes 786436
  25.7 9.5 %copy-start.3 = (s32[24,128]{1,0:T(8,128)S(1)}, s32[24,128]{1,0:T(8,128)}, u32[]{:S(2)}) copy-start(s32[24,128]{1,0:T(8,128)} %get-tuple-element.31.meta_ref) | copy-start | bytes 36868
  25.7 16.7 %all-to-all-start.1 = ((f32[32,3,1,128]{3,2,1,0:T(1,128)}), f32[32,3,1,128]{3,2,1,0:T(1,128)S(1)}, u32[]{:S(2)}, u32[]{:S(2)}) async-start(f32[32,3,1,128]{3,2,1,0:T(1,128)} %bitcast.6), calls=%async_computation.1 | async-start | bytes 98304 | tf_op jit(solution)/shard_map/all_to_all | solution.py:418
  43.0 3.8 %collective-permute-start.3 = (f32[32,128]{1,0:T(8,128)S(1)}, f32[32,128]{1,0:T(8,128)S(1)}, u32[]{:S(2)}, u32[]{:S(2)}) collective-permute-start(f32[32,128]{1,0:T(8,128)S(1)} %get-tuple-element.42.low_ref), channel_id=1, source_target_pairs={{1,0},{2,1},{3,2},{4,3},{5,4},{6,5},{7,6},{0,7},{9,8},{10,9},{11,1... | collective-permute-start | bytes 49160 | tf_op jit(solution)/shard_map/ppermute | solution.py:485
  43.1 3.9 %collective-permute-start.2 = (f32[32,128]{1,0:T(8,128)S(1)}, f32[32,128]{1,0:T(8,128)S(1)}, u32[]{:S(2)}, u32[]{:S(2)}) collective-permute-start(f32[32,128]{1,0:T(8,128)S(1)} %get-tuple-element.43.high_ref), channel_id=1, source_target_pairs={{0,1},{1,2},{2,3},{3,4},{4,5},{5,6},{6,7},{7,0},{8,9},{9,10},{10,1... | collective-permute-start | bytes 49160 | tf_op jit(solution)/shard_map/ppermute | solution.py:484
